TPU v7x, 32 devices: a whole 2x2x4 slice. The times are simulated.
32 devices in a mesh: dp: 32 (over z, y, x, core).
Axes of the slice: x: 2, y: 2, z: 4, core: 2. Of those that a mesh axis runs over, the one named last changes fastest.
Arguments:
- frames: bfloat16 [16384, 768], P('dp'), may hold values from -6 to 6
- ln1_gain: bfloat16 [768], P('dp'), may hold values from 0.5 to 1.5
- ln1_shift: bfloat16 [768], P('dp'), may hold values from -1.75 to 1.75
- w_query: bfloat16 [768, 768], P('dp'), may hold values from -0.21875 to 0.21875
- b_query: bfloat16 [768], P('dp'), may hold values from -3 to 3
- w_key: bfloat16 [768, 768], P('dp'), may hold values from -0.21875 to 0.21875
- w_value: bfloat16 [768, 768], P('dp'), may hold values from -0.21875 to 0.21875
- b_value: bfloat16 [768], P('dp'), may hold values from -1.75 to 1.75
- w_out: bfloat16 [768, 768], P('dp'), may hold values from -2.5 to 2.5
- b_out: bfloat16 [768], P('dp'), may hold values from -1.75 to 1.75
- ln2_gain: bfloat16 [768], P('dp'), may hold values from 0.5 to 1.5
- ln2_shift: bfloat16 [768], P('dp'), may hold values from -1.75 to 1.75
- w_inner: bfloat16 [768, 3072], P('dp'), may hold values from -0.21875 to 0.21875
- b_inner: bfloat16 [3072], P('dp'), may hold values from -3 to 3
- w_outer: bfloat16 [3072, 768], P('dp'), may hold values from -0.109375 to 0.109375
- b_outer: bfloat16 [768], P('dp'), may hold values from -1.75 to 1.75
- bias_table: bfloat16 [3840], P('dp'), may hold values from -6 to 6
- layout: int32 [32], P('dp'), may hold values from 0 to 3, as said below
- valid: int32 [32, 4], P('dp'), may hold values from 65 to 384, as said below
- rel_index: int32 [1023], replicated, may hold values from 0 to 319
- cotangent: bfloat16 [16384, 768], P('dp'), may hold values from -6 to 6
Outputs:
- mixed: bfloat16 [16384, 768], P('dp')
- frames_grad: bfloat16 [16384, 768], P('dp')
- grad_ln1_gain: float32 [768], P('dp')
- grad_ln1_shift: float32 [768], P('dp')
- grad_w_query: float32 [768, 768], P('dp')
- grad_b_query: float32 [768], P('dp')
- grad_w_key: float32 [768, 768], P('dp')
- grad_w_value: float32 [768, 768], P('dp')
- grad_b_value: float32 [768], P('dp')
- grad_w_out: float32 [768, 768], P('dp')
- grad_b_out: float32 [768], P('dp')
- grad_ln2_gain: float32 [768], P('dp')
- grad_ln2_shift: float32 [768], P('dp')
- grad_w_inner: float32 [768, 3072], P('dp')
- grad_b_inner: float32 [3072], P('dp')
- grad_w_outer: float32 [3072, 768], P('dp')
- grad_b_outer: float32 [768], P('dp')
- grad_bias_table: float32 [3840], P('dp')
Inputs may be any that keep to these rules, and one draw needn't show every extreme that they name: `layout`: every code 0 to 3 is taken by some group in every draw. For the s-th sequence of a group, valid holds more than half of its length and at most its length; entries of slots past a group's last sequence are ignored. Some sequence of 384 frames is valid in full in every draw.
All inputs are finite; a program needn't handle non-finite values.
Results may differ from a plain program's by a relative error of at most 0.013.
Values may be sent and summed in bfloat16 or wider, within the bound.
No kernel may reach another device: no remote copies, remote signals or barrier semaphores. Data moves between devices by JAX's collectives and lax.ppermute only.
A program may use at most 192 MiB of HBM per device.

v0:
```python
from functools import partial

import jax
import jax.numpy as jnp
import numpy as np
from jax import lax
from jax.sharding import PartitionSpec as P

HEADS = 12
GROUPS_DEV = 1


segment_units = np.array([[0, 0, 0, 1], [0, 0, 1, 1], [0, 0, 1, 2], [0, 1, 2, 3]], dtype=np.int32)
start_units = np.array([[0, 0, 0, 3], [0, 0, 2, 2], [0, 0, 2, 3], [0, 1, 2, 3]], dtype=np.int32)
masked_score = -1e30


def layer_norm(inputs, gain, shift):
    centred = inputs - jnp.mean(inputs, axis=-1, keepdims=True)
    spread = jnp.mean(centred * centred, axis=-1, keepdims=True)
    return centred * lax.rsqrt(spread + 1e-05) * gain + shift


def toeplitz(vector, length):
    tiled = jnp.tile(vector, length)
    window = lax.slice_in_dim(tiled, length - 1, length - 1 + length * (2 * length - 2))
    return window.reshape(length, 2 * length - 2)[:, :length]


def allowed_pairs(layout_code, slot_valid, unit_rows):
    choose = jnp.arange(4, dtype=jnp.int32)[:, None] == layout_code
    seg_of_unit = jnp.sum(jnp.where(choose, jnp.asarray(segment_units), 0), axis=0).astype(
        jnp.int32
    )
    start_of_unit = jnp.sum(jnp.where(choose, jnp.asarray(start_units), 0), axis=0).astype(
        jnp.int32
    )
    segment = jnp.repeat(seg_of_unit, unit_rows)
    place = (
        jnp.arange(4 * unit_rows, dtype=jnp.int32)
        - jnp.repeat(start_of_unit, unit_rows) * unit_rows
    )
    slot_ids = jnp.arange(4, dtype=jnp.int32)
    limit = jnp.sum(
        jnp.where(segment[:, None] == slot_ids[None, :], slot_valid[None, :], 0), axis=1
    )
    return (segment[:, None] == segment[None, :]) & (place < limit)[None, :]


def packed_pieces(layout_code, slot_valid, unit_rows):
    return [(0, 4 * unit_rows, allowed_pairs(layout_code, slot_valid, unit_rows))]


def head_bias(bias_rows, head_idx, length):
    centre = bias_rows.shape[1] // 2
    return bias_rows[head_idx, centre - length + 1 : centre + length]


def score_block(queries, key_rows, rel_bias, allowed):
    scores = (
        lax.dot_general(
            queries, key_rows, (((1,), (1,)), ((), ())), preferred_element_type=jnp.float32
        )
        + rel_bias
    )
    return jnp.where(allowed, scores, masked_score)


def head_forward(queries, key_rows, values, rel_bias, allowed):
    scores = score_block(queries, key_rows, rel_bias, allowed)
    top_score = jnp.max(scores, axis=1, keepdims=True)
    exp_scores = jnp.exp(scores - top_score)
    totals = jnp.sum(exp_scores, axis=1, keepdims=True)
    weights = (exp_scores / totals).astype(jnp.bfloat16)
    context = jnp.dot(weights, values, preferred_element_type=jnp.float32)
    return (context, (top_score + jnp.log(totals))[:, 0])


def head_backward(queries, key_rows, values, rel_bias, allowed, log_total, grad_context):
    scores = score_block(queries, key_rows, rel_bias, allowed)
    probs = jnp.exp(scores - log_total[:, None])
    weights = probs.astype(jnp.bfloat16)
    grad_values = lax.dot_general(
        weights, grad_context, (((0,), (0,)), ((), ())), preferred_element_type=jnp.float32
    )
    grad_probs = lax.dot_general(
        grad_context, values, (((1,), (1,)), ((), ())), preferred_element_type=jnp.float32
    )
    grad_scores = (
        probs * (grad_probs - jnp.sum(probs * grad_probs, axis=1, keepdims=True))
    ).astype(jnp.bfloat16)
    grad_queries = jnp.dot(grad_scores, key_rows, preferred_element_type=jnp.float32)
    grad_keys = lax.dot_general(
        grad_scores, queries, (((0,), (0,)), ((), ())), preferred_element_type=jnp.float32
    )
    return (grad_queries, grad_keys, grad_values, grad_scores.astype(jnp.float32))


def attend_forward(queries, key_rows, values, bias_rows, pieces, head_size):
    context_cols = []
    total_rows = []
    for head_idx in range(bias_rows.shape[0]):
        columns = slice(head_idx * head_size, (head_idx + 1) * head_size)
        context_parts = []
        log_parts = []
        for offset, length, allowed in pieces:
            row_range = slice(offset, offset + length)
            rel_bias = toeplitz(head_bias(bias_rows, head_idx, length), length)
            context, log_total = head_forward(
                queries[row_range, columns],
                key_rows[row_range, columns],
                values[row_range, columns],
                rel_bias,
                allowed,
            )
            context_parts.append(context)
            log_parts.append(log_total)
        context_cols.append(context_parts[0])
        total_rows.append(log_parts[0])
    return (jnp.concatenate(context_cols, axis=1).astype(jnp.bfloat16), jnp.stack(total_rows))


def attend_backward(
    queries, key_rows, values, bias_rows, pieces, head_size, log_totals, grad_context
):
    span = bias_rows.shape[1]
    query_cols = []
    key_cols = []
    value_cols = []
    bias_grads = []
    for head_idx in range(bias_rows.shape[0]):
        columns = slice(head_idx * head_size, (head_idx + 1) * head_size)
        query_parts = []
        key_parts = []
        value_parts = []
        row_grad = jnp.zeros((span,), jnp.float32)
        for offset, length, allowed in pieces:
            row_range = slice(offset, offset + length)
            rel_bias, pull_back = jax.vjp(
                partial(toeplitz, length=length), head_bias(bias_rows, head_idx, length)
            )
            query_piece, key_piece, value_piece, bias_piece = head_backward(
                queries[row_range, columns],
                key_rows[row_range, columns],
                values[row_range, columns],
                rel_bias,
                allowed,
                log_totals[head_idx, row_range],
                grad_context[row_range, columns],
            )
            (grad_vector,) = pull_back(bias_piece)
            row_grad = grad_vector
            query_parts.append(query_piece)
            key_parts.append(key_piece)
            value_parts.append(value_piece)
        query_cols.append(query_parts[0])
        key_cols.append(key_parts[0])
        value_cols.append(value_parts[0])
        bias_grads.append(row_grad)
    return (
        jnp.concatenate(query_cols, axis=1),
        jnp.concatenate(key_cols, axis=1),
        jnp.concatenate(value_cols, axis=1),
        jnp.stack(bias_grads),
    )


def transpose_dot(left, right):
    return lax.dot_general(
        left, right, (((0,), (0,)), ((), ())), preferred_element_type=jnp.float32
    )


def back_dot(left, right):
    return lax.dot_general(
        left, right, (((1,), (1,)), ((), ())), preferred_element_type=jnp.float32
    )


def on_device(
    frames,
    ln1_gain,
    ln1_shift,
    w_query,
    b_query,
    w_key,
    w_value,
    b_value,
    w_out,
    b_out,
    ln2_gain,
    ln2_shift,
    w_inner,
    b_inner,
    w_outer,
    b_outer,
    bias_table,
    layout,
    valid,
    rel_index,
    cotangent,
):
    gathered = (
        lax.all_gather(w_query, "dp", axis=0, tiled=True),
        lax.all_gather(w_key, "dp", axis=0, tiled=True),
        lax.all_gather(w_value, "dp", axis=0, tiled=True),
        lax.all_gather(w_out, "dp", axis=0, tiled=True),
        lax.all_gather(w_inner, "dp", axis=0, tiled=True),
        lax.all_gather(w_outer, "dp", axis=0, tiled=True),
        lax.all_gather(ln1_gain, "dp", axis=0, tiled=True),
        lax.all_gather(ln1_shift, "dp", axis=0, tiled=True),
        lax.all_gather(b_query, "dp", axis=0, tiled=True),
        lax.all_gather(b_value, "dp", axis=0, tiled=True),
        lax.all_gather(b_out, "dp", axis=0, tiled=True),
        lax.all_gather(ln2_gain, "dp", axis=0, tiled=True),
        lax.all_gather(ln2_shift, "dp", axis=0, tiled=True),
        lax.all_gather(b_inner, "dp", axis=0, tiled=True),
        lax.all_gather(b_outer, "dp", axis=0, tiled=True),
        lax.all_gather(bias_table, "dp", axis=0, tiled=True),
    )
    (
        query_weight,
        key_weight,
        value_weight,
        out_weight,
        inner_weight,
        outer_weight,
        first_gain,
        first_shift,
        query_bias,
        value_bias,
        out_bias,
        second_gain,
        second_shift,
        inner_bias,
        outer_bias,
        bias_grid,
    ) = gathered
    group_count = GROUPS_DEV
    row_count = frames.shape[0] // group_count
    unit_rows = row_count // 4
    model_width = frames.shape[1]
    head_size = model_width // HEADS
    scale = float(head_size) ** (-0.5)
    bucket_count = bias_grid.shape[0] // HEADS
    one_hot = (rel_index[:, None] == jnp.arange(bucket_count, dtype=jnp.int32)[None, :]).astype(
        jnp.float32
    )
    bias_rows = jnp.dot(
        one_hot,
        bias_grid.astype(jnp.float32).reshape(bucket_count, HEADS),
        precision=lax.Precision.HIGHEST,
        preferred_element_type=jnp.float32,
    ).T
    inputs = frames.astype(jnp.float32)
    normed_in = layer_norm(
        inputs, first_gain.astype(jnp.float32), first_shift.astype(jnp.float32)
    ).astype(jnp.bfloat16)
    queries = (
        (
            jnp.dot(normed_in, query_weight, preferred_element_type=jnp.float32)
            + query_bias.astype(jnp.float32)
        )
        * scale
    ).astype(jnp.bfloat16)
    key_rows = jnp.dot(normed_in, key_weight, preferred_element_type=jnp.float32).astype(
        jnp.bfloat16
    )
    values = (
        jnp.dot(normed_in, value_weight, preferred_element_type=jnp.float32)
        + value_bias.astype(jnp.float32)
    ).astype(jnp.bfloat16)
    group_idx = 0
    layout_code = layout[group_idx]
    slot_valid = valid[group_idx]
    pieces = packed_pieces(layout_code, slot_valid, unit_rows)
    context_part, log_part = attend_forward(queries, key_rows, values, bias_rows, pieces, head_size)
    log_groups = [log_part]
    attended = (
        inputs
        + jnp.dot(context_part, out_weight, preferred_element_type=jnp.float32)
        + out_bias.astype(jnp.float32)
    )
    normed_mid = layer_norm(
        attended, second_gain.astype(jnp.float32), second_shift.astype(jnp.float32)
    ).astype(jnp.bfloat16)
    inner_sum = jnp.dot(
        normed_mid, inner_weight, preferred_element_type=jnp.float32
    ) + inner_bias.astype(jnp.float32)
    activated, gelu_pull = jax.vjp(lambda tensor: jax.nn.gelu(tensor, approximate=False), inner_sum)
    activated = activated.astype(jnp.bfloat16)
    mixed = (
        attended
        + jnp.dot(activated, outer_weight, preferred_element_type=jnp.float32)
        + outer_bias.astype(jnp.float32)
    ).astype(jnp.bfloat16)
    regathered = (
        lax.all_gather(w_query, "dp", axis=0, tiled=True),
        lax.all_gather(w_key, "dp", axis=0, tiled=True),
        lax.all_gather(w_value, "dp", axis=0, tiled=True),
        lax.all_gather(w_out, "dp", axis=0, tiled=True),
        lax.all_gather(w_inner, "dp", axis=0, tiled=True),
        lax.all_gather(w_outer, "dp", axis=0, tiled=True),
        lax.all_gather(ln1_gain, "dp", axis=0, tiled=True),
        lax.all_gather(ln1_shift, "dp", axis=0, tiled=True),
        lax.all_gather(b_query, "dp", axis=0, tiled=True),
        lax.all_gather(b_value, "dp", axis=0, tiled=True),
        lax.all_gather(b_out, "dp", axis=0, tiled=True),
        lax.all_gather(ln2_gain, "dp", axis=0, tiled=True),
        lax.all_gather(ln2_shift, "dp", axis=0, tiled=True),
        lax.all_gather(b_inner, "dp", axis=0, tiled=True),
        lax.all_gather(b_outer, "dp", axis=0, tiled=True),
        lax.all_gather(bias_table, "dp", axis=0, tiled=True),
    )
    (
        query_weight,
        key_weight,
        value_weight,
        out_weight,
        inner_weight,
        outer_weight,
        first_gain,
        first_shift,
        query_bias,
        value_bias,
        out_bias,
        second_gain,
        second_shift,
        inner_bias,
        outer_bias,
        bias_grid,
    ) = regathered
    grad_w_outer = transpose_dot(activated, cotangent)
    grad_b_outer = jnp.sum(cotangent.astype(jnp.float32), axis=0)
    (grad_inner,) = gelu_pull(back_dot(cotangent, outer_weight))
    grad_inner = grad_inner.astype(jnp.bfloat16)
    grad_w_inner = transpose_dot(normed_mid, grad_inner)
    grad_b_inner = jnp.sum(grad_inner.astype(jnp.float32), axis=0)
    grad_mid = back_dot(grad_inner, inner_weight)
    _, second_pull = jax.vjp(
        layer_norm, attended, second_gain.astype(jnp.float32), second_shift.astype(jnp.float32)
    )
    mid_rows, grad_second_gain, grad_second_shift = second_pull(grad_mid)
    grad_attended = cotangent.astype(jnp.float32) + mid_rows
    grad_branch = grad_attended.astype(jnp.bfloat16)
    grad_w_out = transpose_dot(context_part, grad_branch)
    grad_b_out = jnp.sum(grad_branch.astype(jnp.float32), axis=0)
    grad_context = back_dot(grad_branch, out_weight).astype(jnp.bfloat16)
    group_idx = 0
    layout_code = layout[group_idx]
    slot_valid = valid[group_idx]
    pieces = packed_pieces(layout_code, slot_valid, unit_rows)
    query_part, key_part, value_part, rows_part = attend_backward(
        queries, key_rows, values, bias_rows, pieces, head_size, log_groups[group_idx], grad_context
    )
    grad_queries = query_part.astype(jnp.bfloat16) * jnp.bfloat16(scale)
    grad_keys = key_part.astype(jnp.bfloat16)
    grad_values = value_part.astype(jnp.bfloat16)
    grad_w_query = transpose_dot(normed_in, grad_queries)
    grad_b_query = jnp.sum(grad_queries.astype(jnp.float32), axis=0)
    grad_w_key = transpose_dot(normed_in, grad_keys)
    grad_w_value = transpose_dot(normed_in, grad_values)
    grad_b_value = jnp.sum(grad_values.astype(jnp.float32), axis=0)
    grad_in = (
        back_dot(grad_queries, query_weight)
        + back_dot(grad_keys, key_weight)
        + back_dot(grad_values, value_weight)
    )
    _, first_pull = jax.vjp(
        layer_norm, inputs, first_gain.astype(jnp.float32), first_shift.astype(jnp.float32)
    )
    in_rows, grad_first_gain, grad_first_shift = first_pull(grad_in)
    frames_grad = (grad_attended + in_rows).astype(jnp.bfloat16)
    grad_table = jnp.dot(
        one_hot.T, rows_part.T, precision=lax.Precision.HIGHEST, preferred_element_type=jnp.float32
    ).reshape(-1)
    owned = (
        lax.psum_scatter(grad_w_query, "dp", scatter_dimension=0, tiled=True),
        lax.psum_scatter(grad_w_key, "dp", scatter_dimension=0, tiled=True),
        lax.psum_scatter(grad_w_value, "dp", scatter_dimension=0, tiled=True),
        lax.psum_scatter(grad_w_out, "dp", scatter_dimension=0, tiled=True),
        lax.psum_scatter(grad_w_inner, "dp", scatter_dimension=0, tiled=True),
        lax.psum_scatter(grad_w_outer, "dp", scatter_dimension=0, tiled=True),
        lax.psum_scatter(grad_first_gain, "dp", scatter_dimension=0, tiled=True),
        lax.psum_scatter(grad_first_shift, "dp", scatter_dimension=0, tiled=True),
        lax.psum_scatter(grad_b_query, "dp", scatter_dimension=0, tiled=True),
        lax.psum_scatter(grad_b_value, "dp", scatter_dimension=0, tiled=True),
        lax.psum_scatter(grad_b_out, "dp", scatter_dimension=0, tiled=True),
        lax.psum_scatter(grad_second_gain, "dp", scatter_dimension=0, tiled=True),
        lax.psum_scatter(grad_second_shift, "dp", scatter_dimension=0, tiled=True),
        lax.psum_scatter(grad_b_inner, "dp", scatter_dimension=0, tiled=True),
        lax.psum_scatter(grad_b_outer, "dp", scatter_dimension=0, tiled=True),
        lax.psum_scatter(grad_table, "dp", scatter_dimension=0, tiled=True),
    )
    (
        sum_w_query,
        sum_w_key,
        sum_w_value,
        sum_w_out,
        sum_w_inner,
        sum_w_outer,
        sum_first_gain,
        sum_first_shift,
        sum_b_query,
        sum_b_value,
        sum_b_out,
        sum_second_gain,
        sum_second_shift,
        sum_b_inner,
        sum_b_outer,
        sum_table,
    ) = owned
    return (
        mixed,
        frames_grad,
        sum_first_gain,
        sum_first_shift,
        sum_w_query,
        sum_b_query,
        sum_w_key,
        sum_w_value,
        sum_b_value,
        sum_w_out,
        sum_b_out,
        sum_second_gain,
        sum_second_shift,
        sum_w_inner,
        sum_b_inner,
        sum_w_outer,
        sum_b_outer,
        sum_table,
    )


def solution(mesh):
    in_specs = (
        P("dp", None),
        P("dp"),
        P("dp"),
        P("dp", None),
        P("dp"),
        P("dp", None),
        P("dp", None),
        P("dp"),
        P("dp", None),
        P("dp"),
        P("dp"),
        P("dp"),
        P("dp", None),
        P("dp"),
        P("dp", None),
        P("dp"),
        P("dp"),
        P("dp"),
        P("dp", None),
        P(),
        P("dp", None),
    )
    out_specs = (
        P("dp", None),
        P("dp", None),
        P("dp"),
        P("dp"),
        P("dp", None),
        P("dp"),
        P("dp", None),
        P("dp", None),
        P("dp"),
        P("dp", None),
        P("dp"),
        P("dp"),
        P("dp"),
        P("dp", None),
        P("dp"),
        P("dp", None),
        P("dp"),
        P("dp"),
    )
    return jax.shard_map(
        on_device, mesh=mesh, in_specs=in_specs, out_specs=out_specs, check_vma=False
    )
```

profile of v0, /device:TPU:0, one launch (start us, length us, event | category | flops | bytes accessed | tf_op | source)
XLA Modules:
  0.0 1192.9 jit_solution(15721871880209057806)
XLA Ops:
  18.1 42.6 %all-reduce.45 = (bf16[3840]{0:T(1024)(128)(2,1)S(1)}, bf16[768]{0:T(1024)(128)(2,1)S(1)}, bf16[768]{0:T(1024)(128)(2,1)S(1)}, bf16[768]{0:T(1024)(128)(2,1)S(1)...) all-reduce(bf16[3840]{0:T(1024)(128)(2,1)S(1)} %dynamic-update-slic, ...), channel_id=1, replica_groups=mesh['dp'=32] {'dp'}, use_global_device_ids=true, to_apply=%add.27 | all-reduce | flops 13056 | bytes 52224
  225.0 10.8 all-gather.13.cloned.1.call-done
  240.1 61.0 %all-gather.15.cloned.1.call-done = bf16[768,3072]{1,0:T(8,128)(2,1)} async-done(((bf16[24,3072]{1,0:T(8,128)(2,1)}), bf16[768,3072]{1,0:T(8,128)(2,1)}) %all-gather.15.cloned.1.call-update) | async-done | bytes 4718608 | tf_op jit(solution)/shard_map/all_gather | solution.py:208
  301.1 8.4 fusion.254
  309.5 56.9 %all-gather.17.cloned.1.call-done = bf16[3072,768]{1,0:T(8,128)(2,1)} async-done(((bf16[96,768]{1,0:T(8,128)(2,1)}), bf16[3072,768]{1,0:T(8,128)(2,1)}) %all-gather.17.cloned.1.call-update) | async-done | bytes 4718608 | tf_op jit(solution)/shard_map/all_gather | solution.py:209
  366.4 20.0 %convert_reduce_fusion = (f32[3072]{0:T(1024)S(1)}, bf16[512,3072]{1,0:T(8,128)(2,1)S(1)}, f32[512,3072]{1,0:T(8,128)}) fusion(f32[512,3072]{1,0:T(8,128)} %fusion.254, f32[3072]{0:T(1024)S(1)} %convert_element_type.232, bf16[512,768]{1,0:T(8,128)(2,1)} %param.43, bf16[3072,768]{1,0:T(8,128)(2,1)} %all-gather.17.cloned.1.call-done), kind=kOutput, calls=%fused_computation.2 | convolution fusion | flops 2533880832 | bytes 21258240 | tf_op jit(solution)/shard_map/dot_general | solution.py:175
  417.4 3.7 reshape.481
  429.9 3.6 reshape.478
  442.1 3.6 reshape.475
  454.3 3.6 reshape.472
  466.6 3.7 reshape.469
  478.8 3.8 reshape.466
  502.2 3.6 reshape.463
  556.7 6.3 multiply_convert_fusion
  564.7 5.1 fusion.283
  569.9 7.1 fusion.253
  586.2 4.4 reshape.508
  637.9 3.6 reshape.451
  663.9 40.8 %all-reduce.44 = (f32[768]{0:T(1024)S(1)}, f32[768]{0:T(1024)S(1)}, f32[768]{0:T(1024)S(1)}, f32[768]{0:T(1024)S(1)}, f32[768]{0:T(1024)S(1)}, /*index=5*/f32[76...) all-reduce(f32[768]{0:T(1024)S(1)} %get-tuple-element.20, ...), channel_id=2, replica_groups=mesh['dp'=32] {'dp'}, use_global_device_ids=true, to_apply=%region_48.49.clone | all-reduce | flops 13056 | bytes 104448
  710.6 6.9 add_convert_fusion.2
  717.5 80.8 %reduce-scatter.7.cloned.1.call-done = f32[24,768]{1,0:T(8,128)} async-done(((f32[768,768]{1,0:T(8,128)}), f32[24,768]{1,0:T(8,128)}) %reduce-scatter.7.cloned.1.call-update) | async-done | bytes 73744 | tf_op jit(solution)/shard_map/reduce_scatter | solution.py:378
  798.2 104.6 %reduce-scatter.13.cloned.1.call-done = f32[24,768]{1,0:T(8,128)} async-done(((f32[768,768]{1,0:T(8,128)}), f32[24,768]{1,0:T(8,128)}) %reduce-scatter.13.cloned.1.call-update) | async-done | bytes 73744 | tf_op jit(solution)/shard_map/reduce_scatter | solution.py:381
  902.9 141.1 %reduce-scatter.15.cloned.1.call-done = f32[24,3072]{1,0:T(8,128)} async-done(((f32[768,3072]{1,0:T(8,128)}), f32[24,3072]{1,0:T(8,128)}) %reduce-scatter.15.cloned.1.call-update) | async-done | bytes 294928 | tf_op jit(solution)/shard_map/reduce_scatter | solution.py:382
  1044.0 141.8 %reduce-scatter.17.cloned.1.call-done = f32[96,768]{1,0:T(8,128)} async-done(((f32[3072,768]{1,0:T(8,128)}), f32[96,768]{1,0:T(8,128)}) %reduce-scatter.17.cloned.1.call-update) | async-done | bytes 294928 | tf_op jit(solution)/shard_map/reduce_scatter | solution.py:383
  (653 shorter events, 407.8 us)
Async XLA Ops:
  7.3 10.3 copy-start.141
  7.3 10.6 copy-start.142
  7.3 54.4 %copy-start.131 = (s32[1023]{0:T(1024)S(1)}, s32[1023]{0:T(1024)}, u32[]{:S(2)}) copy-start(s32[1023]{0:T(1024)} %param.42) | copy-start | bytes 12280
  7.3 181.6 %all-gather.9.cloned.1.call-start = ((), (), s32[]{:S(2)}) async-start(), calls=%async_computation.7 | async-start | bytes 1216512 | tf_op jit(solution)/shard_map/all_gather | solution.py:205
  8.0 183.1 %all-gather.7.cloned.1.call-start = ((), (), s32[]{:S(2)}) async-start(), calls=%async_computation.6 | async-start | bytes 1216512 | tf_op jit(solution)/shard_map/all_gather | solution.py:204
  8.8 199.8 %all-gather.11.cloned.1.call-start = ((), (), s32[]{:S(2)}) async-start(), calls=%async_computation.8 | async-start | bytes 1216512 | tf_op jit(solution)/shard_map/all_gather | solution.py:206
  9.5 226.3 %all-gather.13.cloned.1.call-start = ((), (), s32[]{:S(2)}) async-start(), calls=%async_computation.9 | async-start | bytes 1216512 | tf_op jit(solution)/shard_map/all_gather | solution.py:207
  10.1 291.0 %all-gather.15.cloned.1.call-start = ((), (), s32[]{:S(2)}) async-start(), calls=%async_computation.10 | async-start | bytes 4866048 | tf_op jit(solution)/shard_map/all_gather | solution.py:208
  10.7 355.7 %all-gather.17.cloned.1.call-start = ((), (), s32[]{:S(2)}) async-start(), calls=%async_computation.11 | async-start | bytes 4866048 | tf_op jit(solution)/shard_map/all_gather | solution.py:209
  11.3 706.2 %reduce-scatter.11.cloned.1.call-start = ((), (), s32[]{:S(2)}) async-start(), calls=%async_computation.14 | async-start | bytes 2433024 | tf_op jit(solution)/shard_map/reduce_scatter | solution.py:380
  60.8 240.3 %copy-start.125 = (f32[768]{0:T(1024)}, f32[768]{0:T(1024)S(1)}, u32[]{:S(2)}) copy-start(f32[768]{0:T(1024)S(1)} %convert_element_type.230) | copy-start | bytes 9220
  193.6 12.6 %copy-start.43 = (bf16[512,768]{1,0:T(8,128)(2,1)}, bf16[512,768]{1,0:T(8,128)(2,1)S(1)}, u32[]{:S(2)}) copy-start(bf16[512,768]{1,0:T(8,128)(2,1)S(1)} %multiply_convert_fusion.1) | copy-start | bytes 2359300
  211.1 12.7 %copy-start.110 = (bf16[512,768]{1,0:T(8,128)(2,1)}, bf16[512,768]{1,0:T(8,128)(2,1)S(1)}, u32[]{:S(2)}) copy-start(bf16[512,768]{1,0:T(8,128)(2,1)S(1)} %add_convert_fusion.4) | copy-start | bytes 2359300
  366.4 20.1 %copy-start.79 = (f32[512,768]{1,0:T(8,128)S(1)}, f32[512,768]{1,0:T(8,128)}, u32[]{:S(2)}) copy-start(f32[512,768]{1,0:T(8,128)} %copy-done.78) | copy-start | bytes 4718596
  366.4 20.1 %copy-start.128 = (bf16[768,3072]{1,0:T(8,128)(2,1)S(1)}, bf16[768,3072]{1,0:T(8,128)(2,1)}, u32[]{:S(2)}) copy-start(bf16[768,3072]{1,0:T(8,128)(2,1)} %all-gather.15.cloned.1.call-done) | copy-start | bytes 14155780
  393.1 17.7 %copy-start.45 = (bf16[512,768]{1,0:T(8,128)(2,1)}, bf16[512,768]{1,0:T(8,128)(2,1)S(1)}, u32[]{:S(2)}) copy-start(bf16[512,768]{1,0:T(8,128)(2,1)S(1)} %convolution_convert_fusion) | copy-start | bytes 2359300
  491.3 226.2 %reduce-scatter.9.cloned.1.call-start = ((), (), s32[]{:S(2)}) async-start(), calls=%async_computation.13 | async-start | bytes 2433024 | tf_op jit(solution)/shard_map/reduce_scatter | solution.py:379
  494.1 11.8 copy-start.54
  519.8 278.5 %reduce-scatter.7.cloned.1.call-start = ((), (), s32[]{:S(2)}) async-start(), calls=%async_computation.12 | async-start | bytes 2433024 | tf_op jit(solution)/shard_map/reduce_scatter | solution.py:378
  530.1 372.8 %reduce-scatter.13.cloned.1.call-start = ((), (), s32[]{:S(2)}) async-start(), calls=%async_computation.15 | async-start | bytes 2433024 | tf_op jit(solution)/shard_map/reduce_scatter | solution.py:381
  541.4 502.6 %reduce-scatter.15.cloned.1.call-start = ((), (), s32[]{:S(2)}) async-start(), calls=%async_computation.16 | async-start | bytes 9732096 | tf_op jit(solution)/shard_map/reduce_scatter | solution.py:382
  577.1 608.8 %reduce-scatter.17.cloned.1.call-start = ((), (), s32[]{:S(2)}) async-start(), calls=%async_computation.17 | async-start | bytes 9732096 | tf_op jit(solution)/shard_map/reduce_scatter | solution.py:383
  662.2 48.4 %copy-start.81 = (f32[512,768]{1,0:T(8,128)S(1)}, f32[512,768]{1,0:T(8,128)}, u32[]{:S(2)}) copy-start(f32[512,768]{1,0:T(8,128)} %copy-done.78) | copy-start | bytes 4718596
  662.3 48.4 %copy-start.124 = (f32[768]{0:T(1024)S(1)}, f32[768]{0:T(1024)}, u32[]{:S(2)}) copy-start(f32[768]{0:T(1024)} %convert_element_type.234) | copy-start | bytes 9220
  (144 other events, 423.4 us)
Sparse Core Ops, SparseCore 0:
  11.0 56.9 all-gather.8
  71.0 53.0 all-gather.6
  126.9 52.9 all-gather.10
  182.7 53.0 all-gather.12
  238.5 62.5 all-gather.14
  303.9 62.4 all-gather.16
  491.4 97.9 reduce-scatter.10
  596.1 97.9 reduce-scatter.8
  700.0 98.1 reduce-scatter.6
  804.8 98.0 reduce-scatter.12
  909.4 134.5 reduce-scatter.14
  1051.3 134.4 reduce-scatter.16
where the time goes:
time: 1200 us; the launch traced here: 1190 us
  waiting for transfers between devices  601 us (50%)
  local copies, waits for them, and re-layouts  273 us (23%)
  matrix products  136 us (11%)
  blocking collectives  83.5 us (7%)
  other arithmetic  82.1 us (7%)
  between operations  17 us (1%)
    reduce_scatter x1, waiting for transfers between devices, on_device(): lax.psum_scatter(grad_w_outer, 'dp', scatter_dimension=0, tiled=True)  142 us
    reduce_scatter x1, waiting for transfers between devices, on_device(): lax.psum_scatter(grad_w_inner, 'dp', scatter_dimension=0, tiled=True)  141 us
    reduce_scatter x1, waiting for transfers between devices, on_device(): lax.psum_scatter(grad_w_out, 'dp', scatter_dimension=0, tiled=True)  105 us
    unnamed x2, blocking collectives  83.5 us
    reduce_scatter x1, waiting for transfers between devices, on_device(): lax.psum_scatter(grad_w_query, 'dp', scatter_dimension=0, tiled=True)  80.8 us
    reshape x24, local copies, waits for them, and re-layouts, toeplitz(): return window.reshape(length, 2 * length - 2)[:, :length]  73.8 us
    unnamed x342, local copies, waits for them, and re-layouts  67 us
    all_gather x1, waiting for transfers between devices, on_device(): lax.all_gather(w_inner, 'dp', axis=0, tiled=True)  61 us
  transfers between devices with their start and end apart: 12, of which 7 were waited for; matrix products, arithmetic and copies ran while one was open for 28% of the time, Pallas kernels for 0%

commit v1 on v0

v1 whole, which is shorter than its diff:
```python
import functools

import jax
import jax.numpy as jnp
import numpy as np
from jax import lax
from jax.experimental import pallas as pl
from jax.experimental.pallas import tpu as pltpu
from jax.sharding import PartitionSpec as P

HEADS = 12
LANES = 128
UNITS = 4
MASKED = -1e30
F32 = jnp.float32
BF16 = jnp.bfloat16
SEGMENT = ((0, 0, 0, 1), (0, 0, 1, 1), (0, 0, 1, 2), (0, 1, 2, 3))
START = ((0, 0, 0, 3), (0, 0, 2, 2), (0, 0, 2, 3), (0, 1, 2, 3))
VMEM_LIMIT = 56 * 1024 * 1024


def bit_orders(n):
    chip = [1 << k for k in range(1, n.bit_length() - 1)]
    low, high = chip[:2], chip[2:][::-1]
    return (high + low, high + low[::-1])


def gather_masks(bits):
    masks = [0]
    for bit in bits:
        masks = masks + [bit ^ m for m in masks]
    return masks


def scatter_masks(bits):
    masks = [0]
    for bit in bits:
        masks = [bit ^ m for m in masks] + masks
    return masks


def pairs(n, by_core):
    return [(i, i ^ by_core[i & 1]) for i in range(n)]


def gather(part, n):
    orders = bit_orders(n)
    held = part[None]
    for step, by_core in enumerate(zip(*orders)):
        got = lax.ppermute(held, "dp", pairs(n, by_core))
        if step < len(orders[0]) - 1:
            held = jnp.concatenate([held, got], axis=0)
    return (held, got, lax.ppermute(held, "dp", pairs(n, (1, 1))), lax.ppermute(got, "dp", pairs(n, (1, 1))))


def scatter(send, keep, n):
    orders = bit_orders(n)
    terms = [(keep, 0), (lax.ppermute(send, "dp", pairs(n, (1, 1))), 0)]
    half = n // 4

    def total(count):
        return sum(lax.slice_in_dim(t, at, at + count).astype(F32) for t, at in terms)

    for by_core in reversed(list(zip(*orders))):
        out = total(half).astype(BF16)
        terms = [(t, at + half) for t, at in terms]
        terms.append((lax.ppermute(out, "dp", pairs(n, by_core)), 0))
        half //= 2
    return total(1)[0]


def plan_tables(n):
    orders = bit_orders(n)
    me = lax.axis_index("dp")
    core = me & 1
    g = np.array([gather_masks(o) for o in orders], np.int32)
    s = np.array([scatter_masks(o) for o in orders], np.int32)
    other = np.array([[list(g[1 - c]).index(m) for m in g[c]] for c in (0, 1)], np.int32)
    inverse = np.zeros((2, n), np.int32)
    for c in (0, 1):
        for i, m in enumerate(s[c]):
            inverse[c, m] = i
    devices = jnp.arange(n, dtype=jnp.int32)
    chip_of = (me ^ jnp.asarray(g)[core]) >> 1
    other_place = jnp.asarray(other)[core]
    plane = devices & 1
    mask = (devices ^ me) & ~1
    scatter_place = jnp.asarray(inverse)[plane, mask]
    return me, core, chip_of, other_place, scatter_place


def assemble_kernel(meta, own0, own1, oth0, oth1, out, *, half):
    core = meta[0]
    i = pl.program_id(0)
    for place in range(2 * half):

        @pl.when(i == place)
        def _(place=place):
            mine = (own0 if place < half else own1)[place % half]
            j = meta[1 + 2 * half + place]
            pick0 = oth0[jnp.minimum(j, half - 1)]
            pick1 = oth1[jnp.maximum(j - half, 0)]
            theirs = jnp.where(j < half, pick0, pick1)
            first = jnp.where(core == 0, mine, theirs)
            second = jnp.where(core == 0, theirs, mine)
            out[0] = jnp.concatenate([first, second], axis=0)


def assemble(parts, plan, n):
    me, core, chip_of, other_place, _ = plan
    own0, own1, oth0, oth1 = parts
    half, rows, cols = own0.shape
    if rows % 8:
        mine = jnp.concatenate([own0, own1])
        theirs = jnp.concatenate([oth0, oth1])[other_place]
        both = jnp.where(core == 0, jnp.stack([mine, theirs], 1), jnp.stack([theirs, mine], 1))
        back = jnp.argsort(chip_of)
        return both[back].reshape(n * rows, cols)
    meta = jnp.concatenate([core[None], chip_of, other_place]).astype(jnp.int32)
    whole = pl.BlockSpec((half, rows, cols), lambda i, m: (0, 0, 0))
    out = pl.pallas_call(
        functools.partial(assemble_kernel, half=half),
        grid_spec=pltpu.PrefetchScalarGridSpec(
            num_scalar_prefetch=1,
            grid=(2 * half,),
            in_specs=[whole] * 4,
            out_specs=pl.BlockSpec((1, 2 * rows, cols), lambda i, m: (m[1 + i], 0, 0)),
        ),
        out_shape=jax.ShapeDtypeStruct((2 * half, 2 * rows, cols), BF16),
        compiler_params=pltpu.CompilerParams(vmem_limit_bytes=VMEM_LIMIT),
        name="assemble",
    )(meta, own0, own1, oth0, oth1)
    return out.reshape(n * rows, cols)


def split_natural(grad, plan, n):
    me, core, _, _, place = plan
    rows = grad.shape[0] // n
    blocks = grad.reshape(n // 2, 2, rows, grad.shape[1])
    mine = jnp.where(core == 0, blocks[:, 0], blocks[:, 1])
    theirs = jnp.where(core == 0, blocks[:, 1], blocks[:, 0])
    both = place.reshape(n // 2, 2)
    my_place = jnp.where(core == 0, both[:, 0], both[:, 1])
    their_place = jnp.where(core == 0, both[:, 1], both[:, 0])
    return theirs[jnp.argsort(their_place)], mine[jnp.argsort(my_place)]


def nn(a, b):
    return jnp.dot(a, b, preferred_element_type=F32)


def nt(a, b):
    return lax.dot_general(a, b, (((1,), (1,)), ((), ())), preferred_element_type=F32)


def tn(a, b):
    return lax.dot_general(a, b, (((0,), (0,)), ((), ())), preferred_element_type=F32)


def normalise(v):
    centred = v - jnp.mean(v, axis=-1, keepdims=True)
    r = lax.rsqrt(jnp.mean(centred * centred, axis=-1, keepdims=True) + 1e-05)
    return centred * r, r


def norm_backward(n, r, gain, e):
    eg = e * gain
    return r * (eg - jnp.mean(eg, axis=-1, keepdims=True) - n * jnp.mean(eg * n, axis=-1, keepdims=True))


def pick(table, code, u):
    out = jnp.int32(table[0][u])
    for c in range(1, 4):
        out = jnp.where(code == c, jnp.int32(table[c][u]), out)
    return out


def unit_range(meta, u, unit):
    code = meta[0]
    segment = pick(SEGMENT, code, u)
    start = pick(START, code, u)
    count = meta[1]
    for s in range(1, 4):
        count = jnp.where(segment == s, meta[1 + s], count)
    window = jnp.minimum(start, 1) * unit
    return start * unit, start * unit + count, window


def skewed(row, unit):
    wide = jnp.broadcast_to(row, (unit, row.shape[1]))
    return pltpu.roll(wide, row.shape[1] - (unit - 1), 1, stride=1, stride_axis=0)


def unskewed_sum(block, unit):
    width = block.shape[1]
    total = None
    for a in range(unit // 8):
        part = block[8 * a : 8 * a + 8]
        shift = (unit - 1 - 8 * a) % width
        part = pltpu.roll(part, shift, 1) if shift else part
        total = part if total is None else total + part
    out = total[0:1]
    for s in range(1, 8):
        out = out + pltpu.roll(total[s : s + 1], width - s, 1)
    return out


def put_blocks(place, core, send, keep, value, first, rows, columns):
    for at in range(value.shape[0] // rows):
        part = value[at * rows : (at + 1) * rows].astype(BF16)
        where = place[first + at]

        @pl.when(core == at % 2)
        def _(part=part, where=where):
            keep[where, :, columns] = part

        @pl.when(core != at % 2)
        def _(part=part, where=where):
            send[where, :, columns] = part


def attend_kernel(meta, frames, wqkv, vec, bias, q_out, k_out, v_out, nin_out, ctx_out, lse_out, base):
    rows, width = frames.shape
    unit = rows // UNITS
    window = rows - unit
    head = width // HEADS
    n, _ = normalise(frames[...].astype(F32))
    nin = (n * vec[0:1, :] + vec[1:2, :]).astype(BF16)
    nin_out[...] = nin
    q_out[...] = ((nn(nin, wqkv[:, 0:width]) + vec[2:3, :]) * (head ** -0.5)).astype(BF16)
    k_out[...] = nn(nin, wqkv[:, width : 2 * width]).astype(BF16)
    v_out[...] = (nn(nin, wqkv[:, 2 * width : 3 * width]) + vec[3:4, :]).astype(BF16)
    ranges = [unit_range(meta, u, unit) for u in range(UNITS)]
    column = lax.broadcasted_iota(jnp.int32, (1, window), 1)
    masks = [
        jnp.where((column + ws >= lo) & (column + ws < hi), 0.0, MASKED).astype(F32) for lo, hi, ws in ranges
    ]
    lane = lax.broadcasted_iota(jnp.int32, (unit, LANES), 1)
    lse_out[...] = jnp.zeros_like(lse_out)

    def pair(hp, carry):
        cols = pl.ds(pl.multiple_of(hp * LANES, LANES), LANES)
        for sub in range(2):
            h = 2 * hp + sub
            base[sub] = skewed(bias[pl.ds(h, 1), :], unit)
        for u in range(UNITS):
            lo, hi, ws = ranges[u]
            win = pl.ds(pl.multiple_of(ws, LANES), window)
            shift = pl.ds(pl.multiple_of(ws + (rows - unit) - u * unit, LANES), window)
            urows = slice(u * unit, (u + 1) * unit)
            kk = k_out[win, cols]
            vv = v_out[win, cols]
            qu = q_out[urows, cols]
            parts = []
            lses = lse_out[urows, :]
            for sub in range(2):
                qs = jnp.where((lane >= head) == bool(sub), qu, jnp.zeros_like(qu))
                s = nt(qs, kk) + (base[sub, :, shift] + masks[u])
                top = jnp.max(s, axis=1, keepdims=True)
                e = jnp.exp(s - top)
                tot = jnp.sum(e, axis=1, keepdims=True)
                parts.append(nn(e.astype(BF16), vv) * (1.0 / tot))
                lses = jnp.where(lane == 2 * hp + sub, top + jnp.log(tot), lses)
            lse_out[urows, :] = lses
            ctx_out[urows, cols] = jnp.where(lane < head, parts[0], parts[1]).astype(BF16)
        return carry

    lax.fori_loop(0, HEADS // 2, pair, 0)


def inner_kernel(
    place, frames, ctx, w_out, w_inner, vec, b_inner, cot, att_out, nmid_out, act_out, slope_out, send, keep, *, rows_ff, direct
):
    width = frames.shape[1]
    attended = frames[...].astype(F32) + nn(ctx[...], w_out[...]) + vec[4:5, :]
    att_out[...] = attended
    n, _ = normalise(attended)
    nmid_out[...] = (n * vec[5:6, :] + vec[6:7, :]).astype(BF16)
    core = place[0]

    def tile(t, carry):
        cols = pl.ds(pl.multiple_of(t * width, LANES), width)
        v = nn(nmid_out[...], w_inner[:, cols]) + b_inner[:, cols]
        phi = 0.5 * (1.0 + lax.erf(v * (0.5**0.5)))
        act = (v * phi).astype(BF16)
        act_out[:, cols] = act
        slope_out[:, cols] = (phi + v * jnp.exp(-0.5 * v * v) * 0.3989422804014327).astype(BF16)
        g = tn(act, cot[...])
        if direct:
            per = width // rows_ff
            for at in range(per):
                part = g[at * rows_ff : (at + 1) * rows_ff].astype(BF16)
                where = place[1 + t * per + at]

                @pl.when(core == at % 2)
                def _(part=part, where=where):
                    keep[where] = part

                @pl.when(core != at % 2)
                def _(part=part, where=where):
                    send[where] = part
        else:
            keep[cols, :] = g.astype(BF16)
        return carry

    lax.fori_loop(0, w_inner.shape[1] // width, tile, 0)


def outer_kernel(
    place, act, slope, nmid, attended, cot, w_outer, w_inner, w_out, ctx, vec,
    mixed_out, gatt_out, gctx_out, send, keep, gb_out, gvec_out, acc, gmid, *, rows, direct,
):
    width = nmid.shape[1]
    core = place[0]
    acc[...] = attended[...] + vec[7:8, :]
    gmid[...] = jnp.zeros_like(gmid)
    nblocks = width // rows

    def blocks(value, cols):
        if not direct:
            keep[:, cols] = value.astype(BF16)
            return
        for at in range(nblocks):
            part = value[at * rows : (at + 1) * rows].astype(BF16)
            where = place[1 + at]

            @pl.when(core == at % 2)
            def _(part=part, where=where):
                keep[where, :, cols] = part

            @pl.when(core != at % 2)
            def _(part=part, where=where):
                send[where, :, cols] = part

    def tile(t, carry):
        cols = pl.ds(pl.multiple_of(t * width, LANES), width)
        wo = w_outer[cols, :]
        acc[...] += nn(act[:, cols], wo)
        gi = (slope[:, cols].astype(F32) * nt(cot[...], wo)).astype(BF16)
        gb_out[:, cols] = jnp.sum(gi.astype(F32), axis=0, keepdims=True)
        gmid[...] += nt(gi, w_inner[:, cols])
        blocks(tn(nmid[...], gi), cols)
        return carry

    lax.fori_loop(0, w_inner.shape[1] // width, tile, 0)
    mixed_out[...] = acc[...].astype(BF16)
    n, r = normalise(attended[...])
    e = gmid[...]
    c32 = cot[...].astype(F32)
    gatt = c32 + norm_backward(n, r, vec[5:6, :], e)
    gatt_out[...] = gatt
    gbr = gatt.astype(BF16)
    gctx_out[...] = nt(gbr, w_out[...]).astype(BF16)
    blocks(tn(ctx[...], gbr), slice(w_inner.shape[1], w_inner.shape[1] + width))
    gvec_out[0:1, :] = jnp.sum(gbr.astype(F32), axis=0, keepdims=True)
    gvec_out[1:2, :] = jnp.sum(e * n, axis=0, keepdims=True)
    gvec_out[2:3, :] = jnp.sum(e, axis=0, keepdims=True)
    gvec_out[3:4, :] = jnp.sum(c32, axis=0, keepdims=True)
    gvec_out[4:8, :] = jnp.zeros_like(gvec_out[4:8, :])


def attend_back_kernel(
    meta, place, q, k, v, lse, ctx, gctx, bias_rev, nin, frames, gatt, wqkv, vec,
    fgrad_out, send, keep, gvec_out, grow_out,
    base, gbase, lse_t, delta_t, kt, dqkv, gk, gv, *, rows_d, direct,
):
    rows, width = frames.shape
    unit = rows // UNITS
    window = rows - unit
    head = width // HEADS
    core = place[0]
    lses = jnp.transpose(lse[...])
    for h in range(HEADS):
        lse_t[h] = lses[h : h + 1]
    prod = gctx[...].astype(F32) * ctx[...].astype(F32)
    sel_row = lax.broadcasted_iota(jnp.int32, (16, width), 0)
    sel_col = lax.broadcasted_iota(jnp.int32, (16, width), 1)
    sel = jnp.where((sel_col >= sel_row * head) & (sel_col < (sel_row + 1) * head), 1.0, 0.0).astype(BF16)
    high = prod.astype(BF16)
    low = (prod - high.astype(F32)).astype(BF16)
    deltas = nt(sel, high) + nt(sel, low)
    for h in range(HEADS):
        delta_t[h] = deltas[h : h + 1]
    ranges = [unit_range(meta, u, unit) for u in range(UNITS)]
    row_at = lax.broadcasted_iota(jnp.int32, (window, LANES), 0)
    lane = lax.broadcasted_iota(jnp.int32, (unit, LANES), 1)
    sub_lane = lax.broadcasted_iota(jnp.int32, (LANES, unit), 0)

    def pair(hp, carry):
        at = pl.multiple_of(hp * LANES, LANES)
        cols = pl.ds(at, LANES)
        kt[...] = jnp.transpose(k[:, cols])
        gk[...] = jnp.zeros_like(gk)
        gv[...] = jnp.zeros_like(gv)
        gbase[...] = jnp.zeros_like(gbase)
        for sub in range(2):
            base[sub] = skewed(bias_rev[pl.ds(2 * hp + sub, 1), :], unit)
        for u in range(UNITS):
            lo, hi, ws = ranges[u]
            ws = pl.multiple_of(ws, LANES)
            win = pl.ds(ws, window)
            urows = slice(u * unit, (u + 1) * unit)
            mask = jnp.where((row_at + ws >= lo) & (row_at + ws < hi), 0.0, MASKED).astype(F32)
            kk = k[win, cols]
            vv = v[win, cols]
            qu = q[urows, cols]
            gu = gctx[urows, cols]
            gk_win = gk[win, :]
            gv_win = gv[win, :]
            gq = []
            for sub in range(2):
                h = 2 * hp + sub
                mine = (lane >= head) == bool(sub)
                qs = jnp.where(mine, qu, jnp.zeros_like(qu))
                gs = jnp.where(mine, gu, jnp.zeros_like(gu))
                offsets = [
                    pl.ds(pl.multiple_of((rows - unit) + u * unit - ws - jb * unit, LANES), unit)
                    for jb in range(UNITS - 1)
                ]
                rel = jnp.concatenate([base[sub, :, o] for o in offsets], axis=0)
                s = nt(kk, qs) + rel + mask
                p = jnp.exp(s - lse_t[h, :, urows])
                gp = nt(vv, gs)
                ds = (p * (gp - delta_t[h, :, urows])).astype(BF16)
                gv_win = gv_win + nn(p.astype(BF16), gs)
                gk_win = gk_win + nn(ds, qs)
                gq.append(nn(kt[:, win], ds))
                d32 = ds.astype(F32)
                for jb, o in enumerate(offsets):
                    gbase[sub, :, o] += d32[jb * unit : (jb + 1) * unit]
            gk[win, :] = gk_win
            gv[win, :] = gv_win
            gq_t = jnp.where(sub_lane < head, gq[0], gq[1])
            dqkv[urows, cols] = jnp.transpose(gq_t).astype(BF16) * BF16(head ** -0.5)
        dqkv[:, pl.ds(width + at, LANES)] = gk[...].astype(BF16)
        dqkv[:, pl.ds(2 * width + at, LANES)] = gv[...].astype(BF16)
        for sub in range(2):
            grow_out[pl.ds(2 * hp + sub, 1), :] = unskewed_sum(gbase[sub], unit)
        return carry

    lax.fori_loop(0, HEADS // 2, pair, 0)
    grad_in = jnp.zeros((rows, width), F32)
    for part in range(3):
        cols = slice(part * width, (part + 1) * width)
        d = dqkv[:, cols]
        grad_in = grad_in + nt(d, wqkv[:, cols])
        g = tn(nin[...], d)
        if direct:
            for at in range(width // rows_d):
                block = g[at * rows_d : (at + 1) * rows_d].astype(BF16)
                where = place[1 + at]

                @pl.when(core == at % 2)
                def _(block=block, where=where):
                    keep[where, :, cols] = block

                @pl.when(core != at % 2)
                def _(block=block, where=where):
                    send[where, :, cols] = block
        else:
            keep[:, cols] = g.astype(BF16)
    n, r = normalise(frames[...].astype(F32))
    fgrad_out[...] = (gatt[...] + norm_backward(n, r, vec[0:1, :], grad_in)).astype(BF16)
    gvec_out[0:1, :] = jnp.sum(grad_in * n, axis=0, keepdims=True)
    gvec_out[1:2, :] = jnp.sum(grad_in, axis=0, keepdims=True)
    gvec_out[2:3, :] = jnp.sum(dqkv[:, 0:width].astype(F32), axis=0, keepdims=True)
    gvec_out[3:4, :] = jnp.sum(dqkv[:, 2 * width :].astype(F32), axis=0, keepdims=True)
    gvec_out[4:8, :] = jnp.zeros_like(gvec_out[4:8, :])


def run_kernel(kernel, name, scalars, arrays, outs, scratch=()):
    spec = pl.BlockSpec(memory_space=pltpu.VMEM)
    smem = pl.BlockSpec(memory_space=pltpu.SMEM)
    return pl.pallas_call(
        kernel,
        in_specs=[smem] * len(scalars) + [spec] * len(arrays),
        out_specs=[spec] * len(outs),
        out_shape=[jax.ShapeDtypeStruct(s, d) for s, d in outs],
        scratch_shapes=list(scratch),
        compiler_params=pltpu.CompilerParams(vmem_limit_bytes=VMEM_LIMIT),
        name=name,
    )(*scalars, *arrays)


def on_device(
    frames, ln1_gain, ln1_shift, w_query, b_query, w_key, w_value, b_value, w_out, b_out, ln2_gain, ln2_shift,
    w_inner, b_inner, w_outer, b_outer, bias_table, layout, valid, rel_index, cotangent, *, n,
):
    rows, width = frames.shape
    rows_d = w_query.shape[0]
    rows_ff = w_outer.shape[0]
    ff = w_inner.shape[1]
    span = rel_index.shape[0]
    plan = plan_tables(n)
    me, core, chip_of, other_place, scatter_place = plan
    direct = rows_d % 8 == 0 and rows_ff % 16 == 0
    place = jnp.concatenate([core[None], scatter_place]).astype(jnp.int32)
    meta = jnp.concatenate([layout, valid.reshape(-1)]).astype(jnp.int32)

    small_d = jnp.stack([ln1_gain, ln1_shift, b_query, b_value, b_out, ln2_gain, ln2_shift, b_outer])
    flat = jnp.concatenate([small_d.reshape(-1), b_inner, bias_table])
    per = flat.shape[0] // rows_d
    small = jnp.pad(flat.reshape(rows_d, per), ((0, 0), (0, LANES - per)))
    first = assemble(gather(jnp.concatenate([w_query, w_key, w_value, small], axis=1), n), plan, n)
    second = assemble(gather(jnp.concatenate([w_inner, w_out], axis=1), n), plan, n)
    third = assemble(gather(w_outer, n), plan, n)
    flats = first[:, 3 * width : 3 * width + per].reshape(n, rows_d * per)
    vec = flats[:, : 8 * rows_d].reshape(n, 8, rows_d).transpose(1, 0, 2).reshape(8, width).astype(F32)
    inner_bias = flats[:, 8 * rows_d : 8 * rows_d + rows_ff].reshape(1, ff).astype(F32)
    table = flats[:, 8 * rows_d + rows_ff :].reshape(-1, HEADS)
    buckets = table.shape[0]
    index = jnp.pad(rel_index, (0, 1), constant_values=-1)
    index_rev = jnp.pad(rel_index[::-1], (0, 1), constant_values=-1)
    ids = jnp.arange(buckets, dtype=jnp.int32)
    hot = (ids[:, None] == index[None, :]).astype(BF16)
    hot_rev = (ids[:, None] == index_rev[None, :]).astype(BF16)
    wide = jnp.pad(table, ((0, 0), (0, 16 - HEADS)))
    bias = tn(wide, hot)
    bias_rev = tn(wide, hot_rev)

    q, k, v, nin, ctx, lse = run_kernel(
        attend_kernel, "attend", [meta], [frames, first, vec, bias],
        [((rows, width), BF16)] * 5 + [((rows, LANES), F32)],
        [pltpu.VMEM((2, rows // UNITS, span + 1), F32)],
    )
    if direct:
        part_ff = [((n // 2, rows_ff, width), BF16)] * 2
        part_io = [((n // 2, rows_d, ff + width), BF16)] * 2
        part_qkv = [((n // 2, rows_d, 3 * width), BF16)] * 2
    else:
        part_ff = [((8, LANES), BF16), ((ff, width), BF16)]
        part_io = [((8, LANES), BF16), ((width, ff + width), BF16)]
        part_qkv = [((8, LANES), BF16), ((width, 3 * width), BF16)]

    def split(send, keep):
        return (send, keep) if direct else split_natural(keep, plan, n)

    w_out_all = second[:, ff:]
    w_inner_all = second[:, :ff]
    attended, nmid, act, slope, ff_send, ff_keep = run_kernel(
        functools.partial(inner_kernel, rows_ff=rows_ff, direct=direct), "inner", [place],
        [frames, ctx, w_out_all, w_inner_all, vec, inner_bias, cotangent],
        [((rows, width), F32), ((rows, width), BF16), ((rows, ff), BF16), ((rows, ff), BF16)] + part_ff,
    )
    sum_outer = scatter(*split(ff_send, ff_keep), n)
    mixed, gatt, gctx, io_send, io_keep, gb_inner, gvec2 = run_kernel(
        functools.partial(outer_kernel, rows=rows_d, direct=direct), "outer", [place],
        [act, slope, nmid, attended, cotangent, third, w_inner_all, w_out_all, ctx, vec],
        [((rows, width), BF16), ((rows, width), F32), ((rows, width), BF16)] + part_io
        + [((1, ff), F32), ((8, width), F32)],
        [pltpu.VMEM((rows, width), F32), pltpu.VMEM((rows, width), F32)],
    )
    sum_io = scatter(*split(io_send, io_keep), n)
    unit = rows // UNITS
    fgrad, qkv_send, qkv_keep, gvec1, grow = run_kernel(
        functools.partial(attend_back_kernel, rows_d=rows_d, direct=direct), "attend_back", [meta, place],
        [q, k, v, lse, ctx, gctx, bias_rev, nin, frames, gatt, first, vec],
        [((rows, width), BF16)] + part_qkv + [((8, width), F32), ((16, span + 1), F32)],
        [
            pltpu.VMEM((2, unit, span + 1), F32),
            pltpu.VMEM((2, unit, span + 1), F32),
            pltpu.VMEM((HEADS, 1, rows), F32),
            pltpu.VMEM((HEADS, 1, rows), F32),
            pltpu.VMEM((LANES, rows), BF16),
            pltpu.VMEM((rows, 3 * width), BF16),
            pltpu.VMEM((rows, LANES), F32),
            pltpu.VMEM((rows, LANES), F32),
        ],
    )
    sum_qkv = scatter(*split(qkv_send, qkv_keep), n)
    gtable = lax.dot_general(
        hot_rev.astype(F32), grow, (((1,), (1,)), ((), ())), precision=lax.Precision.HIGHEST, preferred_element_type=F32
    )[:, :HEADS]
    gsmall = jnp.stack([gvec1[0], gvec1[1], gvec1[2], gvec1[3], gvec2[0], gvec2[1], gvec2[2], gvec2[3]])
    gsmall = gsmall.reshape(8, n, rows_d).transpose(1, 0, 2).reshape(n, 8 * rows_d)
    gflat = jnp.concatenate([gsmall, gb_inner.reshape(n, rows_ff), gtable.reshape(n, -1)], axis=1)
    gflat = jnp.pad(gflat, ((0, 0), (0, -gflat.shape[1] % LANES))).astype(BF16)
    sum_flat = scatter(*split_natural(gflat, plan, n), n)[0]
    vecs = sum_flat[: 8 * rows_d].reshape(8, rows_d)
    sum_b_inner = sum_flat[8 * rows_d : 8 * rows_d + rows_ff]
    sum_table = sum_flat[8 * rows_d + rows_ff : 8 * rows_d + rows_ff + bias_table.shape[0]]
    return (
        mixed, fgrad, vecs[0], vecs[1],
        sum_qkv[:, :width], vecs[2], sum_qkv[:, width : 2 * width], sum_qkv[:, 2 * width :], vecs[3],
        sum_io[:, ff:], vecs[4], vecs[5], vecs[6],
        sum_io[:, :ff], sum_b_inner, sum_outer, vecs[7], sum_table,
    )


def solution(mesh):
    row, two = P("dp"), P("dp", None)
    in_specs = (two, row, row, two, row, two, two, row, two, row, row, row, two, row, two, row, row, row, two, P(), two)
    out_specs = (two, two, row, row, two, row, two, two, row, two, row, row, row, two, row, two, row, row)
    return jax.shard_map(
        functools.partial(on_device, n=mesh.shape["dp"]),
        mesh=mesh, in_specs=in_specs, out_specs=out_specs, check_vma=False,
    )
```

time: 1200 us -> 339 us (0.28)
  waiting for transfers between devices: 601 us -> 125 us
  local copies, waits for them, and re-layouts: 273 us -> 19.2 us
  matrix products: 136 us -> 3.42 us
  Pallas kernels: 0 us -> 120 us
  blocking collectives: 83.5 us -> 0 us
  other arithmetic: 82.1 us -> 22.9 us
  starting transfers between devices: 1.05 us -> 46.3 us
  between operations: 17 us -> 1.76 us
    reduce_scatter x6 -> x0, waiting for transfers between devices: 468 us -> none  [the longest x1 142 us: on_device(): lax.psum_scatter(grad_w_outer, 'dp', scatter_dimension=0, tiled=True)]
    dot_general x92 -> x3, matrix products: 136 us -> 3.42 us  [the longest x2 1.91 us: tn(): lax.dot_general(a, b, (((0,), (0,)), ((), ())), preferred_element_type=F32)]
    all_gather x6 -> x0, waiting for transfers between devices: 129 us -> none  [the longest x1 61 us: on_device(): lax.all_gather(w_inner, 'dp', axis=0, tiled=True)]
    ppermute x0 -> x38, waiting for transfers between devices: none -> 125 us  [the longest x16 67.7 us: scatter(): terms.append((lax.ppermute(out, 'dp', pairs(n, by_core)), 0))]
    pallas_call x0 -> x7, Pallas kernels: none -> 120 us  [the longest x4 90.6 us: run_kernel(): pl.pallas_call(kernel, in_specs=[smem] * len(scalars) + [spec] * len(arra...]
    reshape x38 -> x10, local copies, waits for them, and re-layouts: 109 us -> 0.99 us  [the longest x2 0.23 us: on_device(): gsmall.reshape(8, n, rows_d).transpose(1, 0, 2).reshape(n, 8 * rows_d)]
    unnamed x2 -> x0, blocking collectives: 83.5 us -> none
    unnamed x342 -> x26, local copies, waits for them, and re-layouts: 67 us -> 0.21 us
  transfers between devices with their start and end apart: 12 -> 38, of which waited for: 7 -> 20; matrix products, arithmetic and copies ran while one was open for 28% -> 11% of each run, Pallas kernels for 0% -> 27%
where the time goes in v1:
time: 339 us; the launch traced here: 338 us
  waiting for transfers between devices  125 us (37%)
  Pallas kernels  120 us (35%)
  starting transfers between devices  46.3 us (14%)
  other arithmetic  22.9 us (7%)
  local copies, waits for them, and re-layouts  19.2 us (6%)
  matrix products  3.42 us (1%)
    pallas_call x4, Pallas kernels, run_kernel(): pl.pallas_call(kernel, in_specs=[smem] * len(scalars) + [spec] * len(arra...  90.6 us
    ppermute x16, waiting for transfers between devices, scatter(): terms.append((lax.ppermute(out, 'dp', pairs(n, by_core)), 0))  67.7 us
    ppermute x12, waiting for transfers between devices, gather(): got = lax.ppermute(held, 'dp', pairs(n, by_core))  56.8 us
    pallas_call x3, Pallas kernels, assemble(): pl.pallas_call(functools.partial(assemble_kernel, half=half), grid_spec=p...  29.2 us
    ppermute x16, starting transfers between devices, scatter(): terms.append((lax.ppermute(out, 'dp', pairs(n, by_core)), 0))  19.4 us
    ppermute x12, starting transfers between devices, gather(): got = lax.ppermute(held, 'dp', pairs(n, by_core))  16.5 us
    convert_element_type x16, other arithmetic, scatter(): out = total(half).astype(BF16)  11.2 us
    ppermute x3, starting transfers between devices, gather(): lax.ppermute(got, 'dp', pairs(n, (1, 1)))  9.52 us
  transfers between devices with their start and end apart: 38, of which 20 were waited for; matrix products, arithmetic and copies ran while one was open for 11% of the time, Pallas kernels for 27%

profile of v1, /device:TPU:0, one launch (start us, length us, event | category | flops | bytes accessed | tf_op | source)
XLA Modules:
  0.0 338.5 jit_solution(5176093389531598317)
XLA Ops:
  1.6 4.1 %collective-permute-start.6 = (bf16[1,24,3840]{2,1,0:T(8,128)(2,1)S(1)}, bf16[1,24,3840]{2,1,0:T(8,128)(2,1)S(1)}, u32[]{:S(2)}, u32[]{:S(2)}) collective-permute-start(bf16[1,24,3840]{2,1,0:T(8,128)(2,1)S(1)} %maximum_bitcast_fusion), channel_id=1, source_target_pairs={{0,16},{1,17},{2,18},{3,19},{4,20},{5,21},{6,22},{7,23},{8,24},{9,... | collective-permute-start | bytes 552968 | tf_op jit(solution)/shard_map/ppermute | solution.py:50
  6.6 7.7 %collective-permute-done.6 = bf16[1,24,3840]{2,1,0:T(8,128)(2,1)S(1)} collective-permute-done((bf16[1,24,3840]{2,1,0:T(8,128)(2,1)S(1)}, bf16[1,24,3840]{2,1,0:T(8,128)(2,1)S(1)}, u32[]{:S(2)}, u32[]{:S(2)}) %collective-permute-start.6) | collective-permute-done | bytes 184352 | tf_op jit(solution)/shard_map/ppermute | solution.py:50
  20.3 9.5 %collective-permute-done.7 = bf16[2,24,3840]{2,1,0:T(8,128)(2,1)S(1)} collective-permute-done((bf16[2,24,3840]{2,1,0:T(8,128)(2,1)S(1)}, bf16[2,24,3840]{2,1,0:T(8,128)(2,1)S(1)}, u32[]{:S(2)}, u32[]{:S(2)}) %collective-permute-start.7) | collective-permute-done | bytes 368672 | tf_op jit(solution)/shard_map/ppermute | solution.py:50
  33.5 6.4 %collective-permute-done.1 = bf16[2,24,2432]{2,1,0:T(8,128)(2,1)S(1)} collective-permute-done((bf16[2,24,2432]{2,1,0:T(8,128)(2,1)S(1)}, bf16[2,24,2432]{2,1,0:T(8,128)(2,1)S(1)}, u32[]{:S(2)}, u32[]{:S(2)}) %collective-permute-start.1) | collective-permute-done | bytes 233504 | tf_op jit(solution)/shard_map/ppermute | solution.py:50
  45.6 8.0 %collective-permute-done.2 = bf16[4,24,2432]{2,1,0:T(8,128)(2,1)S(1)} collective-permute-done((bf16[4,24,2432]{2,1,0:T(8,128)(2,1)S(1)}, bf16[4,24,2432]{2,1,0:T(8,128)(2,1)S(1)}, u32[]{:S(2)}, u32[]{:S(2)}) %collective-permute-start.2) | collective-permute-done | bytes 466976 | tf_op jit(solution)/shard_map/ppermute | solution.py:50
  55.4 10.8 %collective-permute-done.14 = bf16[4,96,768]{2,1,0:T(8,128)(2,1)S(1)} collective-permute-done((bf16[4,96,768]{2,1,0:T(8,128)(2,1)S(1)}, bf16[4,96,768]{2,1,0:T(8,128)(2,1)S(1)}, u32[]{:S(2)}, u32[]{:S(2)}) %collective-permute-start.14) | collective-permute-done | bytes 589856 | tf_op jit(solution)/shard_map/ppermute | solution.py:50
  67.1 9.0 %collective-permute-done.3.own1 = bf16[8,24,2432]{2,1,0:T(8,128)(2,1)} collective-permute-done((bf16[8,24,2432]{2,1,0:T(8,128)(2,1)}, bf16[8,24,2432]{2,1,0:T(8,128)(2,1)}, u32[]{:S(2)}, u32[]{:S(2)}) %collective-permute-start.3) | collective-permute-done | bytes 933920 | tf_op jit(solution)/shard_map/ppermute | solution.py:50
  76.1 4.7 %collective-permute-start.5 = (bf16[8,24,2432]{2,1,0:T(8,128)(2,1)}, bf16[8,24,2432]{2,1,0:T(8,128)(2,1)}, u32[]{:S(2)}, u32[]{:S(2)}) collective-permute-start(bf16[8,24,2432]{2,1,0:T(8,128)(2,1)} %collective-permute-done.3.own1), channel_id=1, source_target_pairs={{0,1},{1,0},{2,3},{3,2},{4,5},{5,4},{6,7},{7,6},{8,9},{9,8},{10,11... | collective-permute-start | bytes 2801672 | tf_op jit(solution)/shard_map/ppermute | solution.py:53
  88.7 4.4 %collective-permute-start.17 = (bf16[8,96,768]{2,1,0:T(8,128)(2,1)}, bf16[8,96,768]{2,1,0:T(8,128)(2,1)}, u32[]{:S(2)}, u32[]{:S(2)}) collective-permute-start(bf16[8,96,768]{2,1,0:T(8,128)(2,1)} %collective-permute-done.15.own1), channel_id=1, source_target_pairs={{0,1},{1,0},{2,3},{3,2},{4,5},{5,4},{6,7},{7,6},{8,9},{9,8},{10,11... | collective-permute-start | bytes 3538952 | tf_op jit(solution)/shard_map/ppermute | solution.py:53
  95.1 9.2 %assemble.3 = bf16[16,48,2432]{2,1,0:T(8,128)(2,1)} custom-call(s32[33]{0:T(128)} %pad_add_fusion.2.meta, bf16[8,24,2432]{2,1,0:T(8,128)(2,1)} %pad_maximum_fusion.2.own0, bf16[8,24,2432]{2,1,0:T(8,128)(2,1)} %collective-permute-done.3.own1, bf16[8,24,2432]{2,1,0:T(8,128)(2,1)} %collective-permute-done.4.oth0, bf16[8,24,2432]{2,1,0:T(8,128)(2,1)} %collective-permute-done.5.oth1), custom_call_target="tpu_custom_call" | custom-call | tf_op jit(solution)/shard_map/assemble/pallas_call | solution.py:121
  108.2 19.7 %attend.1 = (bf16[512,768]{1,0:T(8,128)(2,1)}, bf16[512,768]{1,0:T(8,128)(2,1)}, bf16[512,768]{1,0:T(8,128)(2,1)}, bf16[512,768]{1,0:T(8,128)(2,1)}, bf16[512,768]{1,0:T(8,128)(2,1)}, /*index=5*/f32[512,128]{1,0:T(8,128)}) custom-call(s32[5]{0:T(128)} %pad_add_fusion.1.meta, bf16[512,768]{1,0:T(8,128)(2,1)} %frames.5, bf16[768,2432]{1,0:T(8,128)(2,1)} %bitcast.90, ...), custom_call_target="tpu_custom_call" | custom-call | tf_op jit(solution)/shard_map/attend/pallas_call | solution.py:474
  128.9 9.5 %assemble.5 = bf16[16,192,768]{2,1,0:T(8,128)(2,1)} custom-call(s32[33]{0:T(128)} %pad_add_fusion.2.meta, bf16[8,96,768]{2,1,0:T(8,128)(2,1)} %copy-done.2, bf16[8,96,768]{2,1,0:T(8,128)(2,1)} %collective-permute-done.15.own1, bf16[8,96,768]{2,1,0:T(8,128)(2,1)} %collective-permute-done.16.oth0, bf16[8,96,768]{2,1,0:T(8,128)(2,1)} %collective-permute-done.17.oth1), custom_call_target="tpu_custom_call" | custom-call | tf_op jit(solution)/shard_map/assemble/pallas_call | solution.py:121
  138.4 10.4 %assemble.4 = bf16[16,48,3840]{2,1,0:T(8,128)(2,1)} custom-call(s32[33]{0:T(128)} %pad_add_fusion.2.meta, bf16[8,24,3840]{2,1,0:T(8,128)(2,1)} %copy-done.1, bf16[8,24,3840]{2,1,0:T(8,128)(2,1)} %collective-permute-done.9.own1, bf16[8,24,3840]{2,1,0:T(8,128)(2,1)} %collective-permute-done.10.oth0, bf16[8,24,3840]{2,1,0:T(8,128)(2,1)} %collective-permute-done.11.oth1), custom_call_target="tpu_custom_call" | custom-call | tf_op jit(solution)/shard_map/assemble/pallas_call | solution.py:121
  148.8 4.8 %slice.472.w_inner = bf16[768,3072]{1,0:T(8,128)(2,1)} slice(bf16[768,3840]{1,0:T(8,128)(2,1)} %bitcast.92), slice={[0:768], [0:3072]} | slice | bytes 9437184 | tf_op jit(solution)/shard_map/slice | solution.py:539
  156.0 18.2 %inner.1 = (f32[512,768]{1,0:T(8,128)}, bf16[512,768]{1,0:T(8,128)(2,1)}, bf16[512,3072]{1,0:T(8,128)(2,1)}, bf16[512,3072]{1,0:T(8,128)(2,1)}, bf16[16,96,768]{...) custom-call(s32[33]{0:T(128)} %pad_add_fusion.place, bf16[512,768]{1,0:T(8,128)(2,1)} %frames.5, ...), custom_call_target="tpu_custom_call" | custom-call | tf_op jit(solution)/shard_map/inner/pallas_call | solution.py:474
  174.2 25.5 %outer.1 = (bf16[512,768]{1,0:T(8,128)(2,1)}, f32[512,768]{1,0:T(8,128)}, bf16[512,768]{1,0:T(8,128)(2,1)}, bf16[16,24,3840]{2,1,0:T(8,128)(2,1)}, bf16[16,24,38...) custom-call(s32[33]{0:T(128)} %pad_add_fusion.place, bf16[512,3072]{1,0:T(8,128)(2,1)} %get-tuple-element.45.act, ...), custom_call_target="tpu_custom_call" | custom-call | tf_op jit(solution)/shard_map/outer/pallas_call | solution.py:474
  199.8 27.2 %attend_back.1 = (bf16[512,768]{1,0:T(8,128)(2,1)}, bf16[16,24,2304]{2,1,0:T(8,128)(2,1)}, bf16[16,24,2304]{2,1,0:T(8,128)(2,1)}, f32[8,768]{1,0:T(8,128)}, f32[16,1024]{1,0:T(8,128)}) custom-call(s32[5]{0:T(128)} %pad_add_fusion.1.meta, s32[33]{0:T(128)} %pad_add_fusion.place, bf16[512,768]{1,0:T(8,128)(2,1)} %get-tuple-element.50.q, ...), custom_call_target="tpu_custom_call" | custom-call | tf_op jit(solution)/shard_map/attend_back/pallas_call | solution.py:474
  253.3 8.2 %collective-permute-done.24 = bf16[8,24,2304]{2,1,0:T(8,128)(2,1)S(1)} collective-permute-done((bf16[8,24,2304]{2,1,0:T(8,128)(2,1)S(1)}, bf16[8,24,2304]{2,1,0:T(8,128)(2,1)S(1)}, u32[]{:S(2)}, u32[]{:S(2)}) %collective-permute-start.24) | collective-permute-done | bytes 884768 | tf_op jit(solution)/shard_map/ppermute | solution.py:67
  265.3 10.5 %collective-permute-done.25 = bf16[4,24,2304]{2,1,0:T(8,128)(2,1)S(1)} collective-permute-done((bf16[4,24,2304]{2,1,0:T(8,128)(2,1)S(1)}, bf16[4,24,2304]{2,1,0:T(8,128)(2,1)S(1)}, u32[]{:S(2)}, u32[]{:S(2)}) %collective-permute-start.25) | collective-permute-done | bytes 442400 | tf_op jit(solution)/shard_map/ppermute | solution.py:67
  279.8 4.5 %collective-permute-done.26 = bf16[2,24,2304]{2,1,0:T(8,128)(2,1)S(1)} collective-permute-done((bf16[2,24,2304]{2,1,0:T(8,128)(2,1)S(1)}, bf16[2,24,2304]{2,1,0:T(8,128)(2,1)S(1)}, u32[]{:S(2)}, u32[]{:S(2)}) %collective-permute-start.26) | collective-permute-done | bytes 221216 | tf_op jit(solution)/shard_map/ppermute | solution.py:67
  288.7 17.9 %collective-permute-done.29 = bf16[8,24,3840]{2,1,0:T(8,128)(2,1)S(1)} collective-permute-done((bf16[8,24,3840]{2,1,0:T(8,128)(2,1)S(1)}, bf16[8,24,3840]{2,1,0:T(8,128)(2,1)S(1)}, u32[]{:S(2)}, u32[]{:S(2)}) %collective-permute-start.29) | collective-permute-done | bytes 1474592 | tf_op jit(solution)/shard_map/ppermute | solution.py:67
  312.3 6.1 %collective-permute-done.30 = bf16[4,24,3840]{2,1,0:T(8,128)(2,1)S(1)} collective-permute-done((bf16[4,24,3840]{2,1,0:T(8,128)(2,1)S(1)}, bf16[4,24,3840]{2,1,0:T(8,128)(2,1)S(1)}, u32[]{:S(2)}, u32[]{:S(2)}) %collective-permute-start.30) | collective-permute-done | bytes 737312 | tf_op jit(solution)/shard_map/ppermute | solution.py:67
  323.2 5.5 %collective-permute-done.31 = bf16[2,24,3840]{2,1,0:T(8,128)(2,1)S(1)} collective-permute-done((bf16[2,24,3840]{2,1,0:T(8,128)(2,1)S(1)}, bf16[2,24,3840]{2,1,0:T(8,128)(2,1)S(1)}, u32[]{:S(2)}, u32[]{:S(2)}) %collective-permute-start.31) | collective-permute-done | bytes 368672 | tf_op jit(solution)/shard_map/ppermute | solution.py:67
  332.2 4.7 %collective-permute-done.32 = bf16[1,24,3840]{2,1,0:T(8,128)(2,1)S(1)} collective-permute-done((bf16[1,24,3840]{2,1,0:T(8,128)(2,1)S(1)}, bf16[1,24,3840]{2,1,0:T(8,128)(2,1)S(1)}, u32[]{:S(2)}, u32[]{:S(2)}) %collective-permute-start.32) | collective-permute-done | bytes 184352 | tf_op jit(solution)/shard_map/ppermute | solution.py:67
  (174 shorter events, 90.0 us)
Async XLA Ops:
  14.3 15.5 %collective-permute-start.7 = (bf16[2,24,3840]{2,1,0:T(8,128)(2,1)S(1)}, bf16[2,24,3840]{2,1,0:T(8,128)(2,1)S(1)}, u32[]{:S(2)}, u32[]{:S(2)}) collective-permute-start(bf16[2,24,3840]{2,1,0:T(8,128)(2,1)S(1)} %pad_maximum_fusion.6), channel_id=1, source_target_pairs={{0,8},{1,9},{2,10},{3,11},{4,12},{5,13},{6,14},{7,15},{8,0},{9,1},... | collective-permute-start | bytes 1105928 | tf_op jit(solution)/shard_map/ppermute | solution.py:50
  16.8 14.4 %collective-permute-start = (bf16[1,24,2432]{2,1,0:T(8,128)(2,1)S(1)}, bf16[1,24,2432]{2,1,0:T(8,128)(2,1)S(1)}, u32[]{:S(2)}, u32[]{:S(2)}) collective-permute-start(bf16[1,24,2432]{2,1,0:T(8,128)(2,1)S(1)} %fusion.8), channel_id=1, source_target_pairs={{0,16},{1,17},{2,18},{3,19},{4,20},{5,21},{6,22},{7,23},{8,24},{9,... | collective-permute-start | bytes 350216 | tf_op jit(solution)/shard_map/ppermute | solution.py:50
  29.9 14.8 %collective-permute-start.8 = (bf16[4,24,3840]{2,1,0:T(8,128)(2,1)S(1)}, bf16[4,24,3840]{2,1,0:T(8,128)(2,1)S(1)}, u32[]{:S(2)}, u32[]{:S(2)}) collective-permute-start(bf16[4,24,3840]{2,1,0:T(8,128)(2,1)S(1)} %pad_maximum_fusion.3), channel_id=1, source_target_pairs={{0,2},{1,5},{2,0},{3,7},{4,6},{5,1},{6,4},{7,3},{8,10},{9,13},{10,... | collective-permute-start | bytes 2211848 | tf_op jit(solution)/shard_map/ppermute | solution.py:50
  40.0 13.6 %collective-permute-start.2 = (bf16[4,24,2432]{2,1,0:T(8,128)(2,1)S(1)}, bf16[4,24,2432]{2,1,0:T(8,128)(2,1)S(1)}, u32[]{:S(2)}, u32[]{:S(2)}) collective-permute-start(bf16[4,24,2432]{2,1,0:T(8,128)(2,1)S(1)} %pad_maximum_fusion.5), channel_id=1, source_target_pairs={{0,2},{1,5},{2,0},{3,7},{4,6},{5,1},{6,4},{7,3},{8,10},{9,13},{10,... | collective-permute-start | bytes 1400840 | tf_op jit(solution)/shard_map/ppermute | solution.py:50
  43.1 23.1 %collective-permute-start.14 = (bf16[4,96,768]{2,1,0:T(8,128)(2,1)S(1)}, bf16[4,96,768]{2,1,0:T(8,128)(2,1)S(1)}, u32[]{:S(2)}, u32[]{:S(2)}) collective-permute-start(bf16[4,96,768]{2,1,0:T(8,128)(2,1)S(1)} %pad_maximum_fusion.4), channel_id=1, source_target_pairs={{0,2},{1,5},{2,0},{3,7},{4,6},{5,1},{6,4},{7,3},{8,10},{9,13},{10,... | collective-permute-start | bytes 1769480 | tf_op jit(solution)/shard_map/ppermute | solution.py:50
  44.8 37.1 %collective-permute-start.9 = (bf16[8,24,3840]{2,1,0:T(8,128)(2,1)S(1)}, bf16[8,24,3840]{2,1,0:T(8,128)(2,1)}, u32[]{:S(2)}, u32[]{:S(2)}) collective-permute-start(bf16[8,24,3840]{2,1,0:T(8,128)(2,1)S(1)} %pad_maximum_fusion.own0), channel_id=1, source_target_pairs={{0,4},{1,3},{2,6},{3,1},{4,0},{5,7},{6,2},{7,5},{8,12},{9,11},{10,... | collective-permute-start | bytes 4423688 | tf_op jit(solution)/shard_map/ppermute | solution.py:50
  54.7 21.4 %collective-permute-start.3 = (bf16[8,24,2432]{2,1,0:T(8,128)(2,1)}, bf16[8,24,2432]{2,1,0:T(8,128)(2,1)}, u32[]{:S(2)}, u32[]{:S(2)}) collective-permute-start(bf16[8,24,2432]{2,1,0:T(8,128)(2,1)} %pad_maximum_fusion.2.own0), channel_id=1, source_target_pairs={{0,4},{1,3},{2,6},{3,1},{4,0},{5,7},{6,2},{7,5},{8,12},{9,11},{10,... | collective-permute-start | bytes 2801672 | tf_op jit(solution)/shard_map/ppermute | solution.py:50
  66.4 22.3 %collective-permute-start.15 = (bf16[8,96,768]{2,1,0:T(8,128)(2,1)S(1)}, bf16[8,96,768]{2,1,0:T(8,128)(2,1)}, u32[]{:S(2)}, u32[]{:S(2)}) collective-permute-start(bf16[8,96,768]{2,1,0:T(8,128)(2,1)S(1)} %pad_maximum_fusion.1.own0), channel_id=1, source_target_pairs={{0,4},{1,3},{2,6},{3,1},{4,0},{5,7},{6,2},{7,5},{8,12},{9,11},{10,... | collective-permute-start | bytes 3538952 | tf_op jit(solution)/shard_map/ppermute | solution.py:50
  67.1 18.4 %collective-permute-start.4 = (bf16[8,24,2432]{2,1,0:T(8,128)(2,1)}, bf16[8,24,2432]{2,1,0:T(8,128)(2,1)}, u32[]{:S(2)}, u32[]{:S(2)}) collective-permute-start(bf16[8,24,2432]{2,1,0:T(8,128)(2,1)} %pad_maximum_fusion.2.own0), channel_id=1, source_target_pairs={{0,1},{1,0},{2,3},{3,2},{4,5},{5,4},{6,7},{7,6},{8,9},{9,8},{10,11... | collective-permute-start | bytes 2801672 | tf_op jit(solution)/shard_map/ppermute | solution.py:53
  76.1 19.0 %collective-permute-start.5 = (bf16[8,24,2432]{2,1,0:T(8,128)(2,1)}, bf16[8,24,2432]{2,1,0:T(8,128)(2,1)}, u32[]{:S(2)}, u32[]{:S(2)}) collective-permute-start(bf16[8,24,2432]{2,1,0:T(8,128)(2,1)} %collective-permute-done.3.own1), channel_id=1, source_target_pairs={{0,1},{1,0},{2,3},{3,2},{4,5},{5,4},{6,7},{7,6},{8,9},{9,8},{10,11... | collective-permute-start | bytes 2801672 | tf_op jit(solution)/shard_map/ppermute | solution.py:53
  81.8 56.5 %collective-permute-start.10 = (bf16[8,24,3840]{2,1,0:T(8,128)(2,1)S(1)}, bf16[8,24,3840]{2,1,0:T(8,128)(2,1)}, u32[]{:S(2)}, u32[]{:S(2)}) collective-permute-start(bf16[8,24,3840]{2,1,0:T(8,128)(2,1)S(1)} %pad_maximum_fusion.own0), channel_id=1, source_target_pairs={{0,1},{1,0},{2,3},{3,2},{4,5},{5,4},{6,7},{7,6},{8,9},{9,8},{10,11... | collective-permute-start | bytes 4423688 | tf_op jit(solution)/shard_map/ppermute | solution.py:53
  81.9 56.5 %collective-permute-start.11 = (bf16[8,24,3840]{2,1,0:T(8,128)(2,1)}, bf16[8,24,3840]{2,1,0:T(8,128)(2,1)}, u32[]{:S(2)}, u32[]{:S(2)}) collective-permute-start(bf16[8,24,3840]{2,1,0:T(8,128)(2,1)} %collective-permute-done.9.own1), channel_id=1, source_target_pairs={{0,1},{1,0},{2,3},{3,2},{4,5},{5,4},{6,7},{7,6},{8,9},{9,8},{10,11... | collective-permute-start | bytes 4423688 | tf_op jit(solution)/shard_map/ppermute | solution.py:53
  85.5 43.4 %collective-permute-start.16 = (bf16[8,96,768]{2,1,0:T(8,128)(2,1)S(1)}, bf16[8,96,768]{2,1,0:T(8,128)(2,1)}, u32[]{:S(2)}, u32[]{:S(2)}) collective-permute-start(bf16[8,96,768]{2,1,0:T(8,128)(2,1)S(1)} %pad_maximum_fusion.1.own0), channel_id=1, source_target_pairs={{0,1},{1,0},{2,3},{3,2},{4,5},{5,4},{6,7},{7,6},{8,9},{9,8},{10,11... | collective-permute-start | bytes 3538952 | tf_op jit(solution)/shard_map/ppermute | solution.py:53
  88.7 40.1 %collective-permute-start.17 = (bf16[8,96,768]{2,1,0:T(8,128)(2,1)}, bf16[8,96,768]{2,1,0:T(8,128)(2,1)}, u32[]{:S(2)}, u32[]{:S(2)}) collective-permute-start(bf16[8,96,768]{2,1,0:T(8,128)(2,1)} %collective-permute-done.15.own1), channel_id=1, source_target_pairs={{0,1},{1,0},{2,3},{3,2},{4,5},{5,4},{6,7},{7,6},{8,9},{9,8},{10,11... | collective-permute-start | bytes 3538952 | tf_op jit(solution)/shard_map/ppermute | solution.py:53
  174.2 76.6 %collective-permute-start.33 = (bf16[16,96,768]{2,1,0:T(8,128)(2,1)}, bf16[16,96,768]{2,1,0:T(8,128)(2,1)}, u32[]{:S(2)}, u32[]{:S(2)}) collective-permute-start(bf16[16,96,768]{2,1,0:T(8,128)(2,1)} %get-tuple-element.69), channel_id=1, source_target_pairs={{0,1},{1,0},{2,3},{3,2},{4,5},{5,4},{6,7},{7,6},{8,9},{9,8},{10,11... | collective-permute-start | bytes 7077896 | tf_op jit(solution)/shard_map/ppermute | solution.py:58
  227.0 19.4 %collective-permute-start.23 = (bf16[16,24,2304]{2,1,0:T(8,128)(2,1)}, bf16[16,24,2304]{2,1,0:T(8,128)(2,1)}, u32[]{:S(2)}, u32[]{:S(2)}) collective-permute-start(bf16[16,24,2304]{2,1,0:T(8,128)(2,1)} %get-tuple-element.65), channel_id=1, source_target_pairs={{0,1},{1,0},{2,3},{3,2},{4,5},{5,4},{6,7},{7,6},{8,9},{9,8},{10,11... | collective-permute-start | bytes 5308424 | tf_op jit(solution)/shard_map/ppermute | solution.py:58
  234.6 28.6 %collective-permute-start.28 = (bf16[16,24,3840]{2,1,0:T(8,128)(2,1)}, bf16[16,24,3840]{2,1,0:T(8,128)(2,1)S(1)}, u32[]{:S(2)}, u32[]{:S(2)}) collective-permute-start(bf16[16,24,3840]{2,1,0:T(8,128)(2,1)} %get-tuple-element.67), channel_id=1, source_target_pairs={{0,1},{1,0},{2,3},{3,2},{4,5},{5,4},{6,7},{7,6},{8,9},{9,8},{10,11... | collective-permute-start | bytes 8847368 | tf_op jit(solution)/shard_map/ppermute | solution.py:58
  248.2 13.3 %collective-permute-start.24 = (bf16[8,24,2304]{2,1,0:T(8,128)(2,1)S(1)}, bf16[8,24,2304]{2,1,0:T(8,128)(2,1)S(1)}, u32[]{:S(2)}, u32[]{:S(2)}) collective-permute-start(bf16[8,24,2304]{2,1,0:T(8,128)(2,1)S(1)} %add_convert_fusion.2), channel_id=1, source_target_pairs={{0,4},{1,3},{2,6},{3,1},{4,0},{5,7},{6,2},{7,5},{8,12},{9,11},{10,... | collective-permute-start | bytes 2654216 | tf_op jit(solution)/shard_map/ppermute | solution.py:67
  252.6 33.5 %collective-permute-start.34 = (bf16[8,96,768]{2,1,0:T(8,128)(2,1)S(1)}, bf16[8,96,768]{2,1,0:T(8,128)(2,1)S(1)}, u32[]{:S(2)}, u32[]{:S(2)}) collective-permute-start(bf16[8,96,768]{2,1,0:T(8,128)(2,1)S(1)} %add_convert_fusion.1), channel_id=1, source_target_pairs={{0,4},{1,3},{2,6},{3,1},{4,0},{5,7},{6,2},{7,5},{8,12},{9,11},{10,... | collective-permute-start | bytes 3538952 | tf_op jit(solution)/shard_map/ppermute | solution.py:67
  262.7 13.2 %collective-permute-start.25 = (bf16[4,24,2304]{2,1,0:T(8,128)(2,1)S(1)}, bf16[4,24,2304]{2,1,0:T(8,128)(2,1)S(1)}, u32[]{:S(2)}, u32[]{:S(2)}) collective-permute-start(bf16[4,24,2304]{2,1,0:T(8,128)(2,1)S(1)} %add_convert_fusion.5), channel_id=1, source_target_pairs={{0,2},{1,5},{2,0},{3,7},{4,6},{5,1},{6,4},{7,3},{8,10},{9,13},{10,... | collective-permute-start | bytes 1327112 | tf_op jit(solution)/shard_map/ppermute | solution.py:67
  263.6 43.0 %collective-permute-start.29 = (bf16[8,24,3840]{2,1,0:T(8,128)(2,1)S(1)}, bf16[8,24,3840]{2,1,0:T(8,128)(2,1)S(1)}, u32[]{:S(2)}, u32[]{:S(2)}) collective-permute-start(bf16[8,24,3840]{2,1,0:T(8,128)(2,1)S(1)} %add_convert_fusion), channel_id=1, source_target_pairs={{0,4},{1,3},{2,6},{3,1},{4,0},{5,7},{6,2},{7,5},{8,12},{9,11},{10,... | collective-permute-start | bytes 4423688 | tf_op jit(solution)/shard_map/ppermute | solution.py:67
  285.3 21.7 %collective-permute-start.27 = (bf16[1,24,2304]{2,1,0:T(8,128)(2,1)S(1)}, bf16[1,24,2304]{2,1,0:T(8,128)(2,1)S(1)}, u32[]{:S(2)}, u32[]{:S(2)}) collective-permute-start(bf16[1,24,2304]{2,1,0:T(8,128)(2,1)S(1)} %add_convert_fusion.11), channel_id=1, source_target_pairs={{0,16},{1,17},{2,18},{3,19},{4,20},{5,21},{6,22},{7,23},{8,24},{9,... | collective-permute-start | bytes 331784 | tf_op jit(solution)/shard_map/ppermute | solution.py:67
  287.4 20.6 %collective-permute-start.35 = (bf16[4,96,768]{2,1,0:T(8,128)(2,1)S(1)}, bf16[4,96,768]{2,1,0:T(8,128)(2,1)S(1)}, u32[]{:S(2)}, u32[]{:S(2)}) collective-permute-start(bf16[4,96,768]{2,1,0:T(8,128)(2,1)S(1)} %add_convert_fusion.4), channel_id=1, source_target_pairs={{0,2},{1,5},{2,0},{3,7},{4,6},{5,1},{6,4},{7,3},{8,10},{9,13},{10,... | collective-permute-start | bytes 1769480 | tf_op jit(solution)/shard_map/ppermute | solution.py:67
  309.2 12.9 %collective-permute-start.36 = (bf16[2,96,768]{2,1,0:T(8,128)(2,1)S(1)}, bf16[2,96,768]{2,1,0:T(8,128)(2,1)S(1)}, u32[]{:S(2)}, u32[]{:S(2)}) collective-permute-start(bf16[2,96,768]{2,1,0:T(8,128)(2,1)S(1)} %add_convert_fusion.7), channel_id=1, source_target_pairs={{0,8},{1,9},{2,10},{3,11},{4,12},{5,13},{6,14},{7,15},{8,0},{9,1},... | collective-permute-start | bytes 884744 | tf_op jit(solution)/shard_map/ppermute | solution.py:67
  (26 other events, 448.0 us)

commit v2 on v1

v2 whole, which is shorter than its diff:
```python
import functools
import math

import jax
import jax.numpy as jnp
import numpy as np
from jax import lax
from jax.experimental import pallas as pl
from jax.experimental.pallas import tpu as pltpu
from jax.sharding import PartitionSpec as P

HEADS = 12
LANES = 128
UNITS = 4
MASKED = -1e30
F32 = jnp.float32
BF16 = jnp.bfloat16
SEGMENT = ((0, 0, 0, 1), (0, 0, 1, 1), (0, 0, 1, 2), (0, 1, 2, 3))
START = ((0, 0, 0, 3), (0, 0, 2, 2), (0, 0, 2, 3), (0, 1, 2, 3))
MIB = 1024 * 1024


def bit_orders(n):
    chip = [1 << k for k in range(1, n.bit_length() - 1)]
    low, high = chip[:2], chip[2:][::-1]
    return (high + low, high + low[::-1])


def gather_masks(bits):
    masks = [0]
    for bit in bits:
        masks = masks + [bit ^ m for m in masks]
    return masks


def scatter_masks(bits):
    masks = [0]
    for bit in bits:
        masks = [bit ^ m for m in masks] + masks
    return masks


def pairs(n, by_core):
    return [(i, i ^ by_core[i & 1]) for i in range(n)]


class Order:
    def __init__(self):
        self.last = None

    def after(self, *arrays):
        if self.last is None:
            return arrays
        return lax.optimization_barrier((*arrays, self.last))[:-1]

    def did(self, array):
        self.last = array


class Gather:
    def __init__(self, part, n, order):
        self.n = n
        self.order = order
        self.steps = list(zip(*bit_orders(n)))
        self.held = part[None]
        self.got = lax.ppermute(self.held, "dp", pairs(n, self.steps.pop(0)))

    def step(self):
        pair = self.order.after(self.held, self.got)
        self.held = jnp.concatenate(pair, axis=0)
        self.order.did(self.held)
        self.got = lax.ppermute(self.held, "dp", pairs(self.n, self.steps.pop(0)))
        return self

    def finish(self):
        while self.steps:
            self.step()
        swap = pairs(self.n, (1, 1))
        return (self.held, self.got, lax.ppermute(self.held, "dp", swap), lax.ppermute(self.got, "dp", swap))


class Scatter:
    def __init__(self, n, order):
        self.n = n
        self.order = order
        self.parts = []
        self.terms = []
        self.at = 0
        self.steps = list(reversed(list(zip(*bit_orders(n)))))
        self.half = n // 4

    def add(self, send, keep):
        self.parts.append((keep, lax.ppermute(send, "dp", pairs(self.n, (1, 1)))))
        return self

    def total(self, count, dtype):
        flat = [t for part in self.parts for t in part] + [t for t, _ in self.terms]
        flat = list(self.order.after(*flat))
        at = self.at
        cut = [lax.slice_in_dim(t, at, at + count).astype(F32) for t in flat[: 2 * len(self.parts)]]
        out = [cut[2 * i] + cut[2 * i + 1] for i in range(len(self.parts))]
        out = out[0] if len(out) == 1 else jnp.concatenate(out, axis=-1)
        for t, (_, first) in zip(flat[2 * len(self.parts) :], self.terms):
            out = out + lax.slice_in_dim(t, at - first, at - first + count).astype(F32)
        out = out.astype(dtype)
        self.order.did(out)
        return out

    def step(self):
        by_core = self.steps.pop(0)
        out = self.total(self.half, BF16)
        self.at += self.half
        self.terms.append((lax.ppermute(out, "dp", pairs(self.n, by_core)), self.at))
        self.half //= 2

    def finish(self):
        while self.steps:
            self.step()
        return self.total(1, F32)[0]


def plan_tables(n):
    orders = bit_orders(n)
    me = lax.axis_index("dp")
    core = me & 1
    g = np.array([gather_masks(o) for o in orders], np.int32)
    s = np.array([scatter_masks(o) for o in orders], np.int32)
    inverse = np.zeros((2, n), np.int32)
    for c in (0, 1):
        for i, m in enumerate(s[c]):
            inverse[c, m] = i
    devices = jnp.arange(n, dtype=jnp.int32)
    chips = (me ^ jnp.where(core == 0, jnp.asarray(g[0]), jnp.asarray(g[1]))) >> 1
    mask = (devices ^ me) & ~1
    place = jnp.sum(jnp.where(mask[:, None] == devices[None, :], jnp.asarray(inverse)[np.arange(n) % 2], 0), axis=1)
    return core, chips, place


def crossed_places(n):
    first, second = (gather_masks(o) for o in bit_orders(n))
    places = [second.index(m) for m in first]
    assert places == [first.index(m) for m in second]
    return places


def gathered(parts, plan, n):
    core, chips, _ = plan
    mine = jnp.concatenate(parts[:2])
    theirs = jnp.concatenate(parts[2:])[np.array(crossed_places(n))]
    both = jnp.where(core == 0, jnp.stack([mine, theirs], 1), jnp.stack([theirs, mine], 1))
    return both[jnp.argsort(chips)].reshape(n * mine.shape[1], mine.shape[2])


def split_natural(grad, plan, n):
    core, _, place = plan
    rows = grad.shape[0] // n
    blocks = grad.reshape(n // 2, 2, rows, grad.shape[1])
    mine = jnp.where(core == 0, blocks[:, 0], blocks[:, 1])
    theirs = jnp.where(core == 0, blocks[:, 1], blocks[:, 0])
    both = place.reshape(n // 2, 2)
    my_place = jnp.where(core == 0, both[:, 0], both[:, 1])
    their_place = jnp.where(core == 0, both[:, 1], both[:, 0])
    return theirs[jnp.argsort(their_place)], mine[jnp.argsort(my_place)]


def nn(a, b):
    return jnp.dot(a, b, preferred_element_type=F32)


def nt(a, b):
    return lax.dot_general(a, b, (((1,), (1,)), ((), ())), preferred_element_type=F32)


def tn(a, b):
    return lax.dot_general(a, b, (((0,), (0,)), ((), ())), preferred_element_type=F32)


def normalise(v):
    centred = v - jnp.mean(v, axis=-1, keepdims=True)
    r = lax.rsqrt(jnp.mean(centred * centred, axis=-1, keepdims=True) + 1e-05)
    return centred * r, r


def norm_backward(n, r, gain, e):
    eg = e * gain
    return r * (eg - jnp.mean(eg, axis=-1, keepdims=True) - n * jnp.mean(eg * n, axis=-1, keepdims=True))


def pick(table, code, u):
    out = jnp.int32(table[0][u])
    for c in range(1, 4):
        out = jnp.where(code == c, jnp.int32(table[c][u]), out)
    return out


def unit_range(meta, u, unit):
    code = meta[0]
    segment = pick(SEGMENT, code, u)
    start = pick(START, code, u)
    count = meta[1]
    for s in range(1, 4):
        count = jnp.where(segment == s, meta[1 + s], count)
    window = jnp.minimum(start, 1) * unit
    return start * unit, start * unit + count, window


def skewed(row, unit):
    wide = jnp.broadcast_to(row, (unit, row.shape[1]))
    return pltpu.roll(wide, row.shape[1] - (unit - 1), 1, stride=1, stride_axis=0)


def unskewed_sum(block, unit):
    width = block.shape[1]
    total = None
    for a in range(unit // 8):
        part = block[8 * a : 8 * a + 8]
        shift = (unit - 1 - 8 * a) % width
        part = pltpu.roll(part, shift, 1) if shift else part
        total = part if total is None else total + part
    out = total[0:1]
    for s in range(1, 8):
        out = out + pltpu.roll(total[s : s + 1], width - s, 1)
    return out


def unpack(core, chips, parts, crossed, out, columns):
    half = parts[0].shape[0]
    for i, j in enumerate(crossed):
        mine = parts[i // half][i % half, :, columns]
        theirs = parts[2 + j // half][j % half, :, columns]
        first = jnp.where(core == 0, mine, theirs)
        second = jnp.where(core == 0, theirs, mine)
        out[chips[i]] = jnp.concatenate([first, second], axis=0)


def weight(ref, columns):
    value = ref[..., columns]
    return value.reshape(-1, value.shape[-1])


def put_blocks(core, place, first, value, send, keep, rows, columns):
    for at in range(value.shape[0] // rows):
        part = value[at * rows : (at + 1) * rows].astype(BF16)
        where = place[first + at]

        @pl.when(core == at % 2)
        def _(part=part, where=where):
            keep[where, :, columns] = part

        @pl.when(core != at % 2)
        def _(part=part, where=where):
            send[where, :, columns] = part


def project_body(meta, frames, w, vec, q_out, k_out, v_out, nin_out):
    width = frames.shape[1]
    head = width // HEADS
    n, _ = normalise(frames[...].astype(F32))
    nin = (n * vec[0:1, :] + vec[1:2, :]).astype(BF16)
    nin_out[...] = nin
    q_out[...] = ((nn(nin, weight(w, slice(0, width))) + vec[2:3, :]) * (head**-0.5)).astype(BF16)
    k_out[...] = nn(nin, weight(w, slice(width, 2 * width))).astype(BF16)
    v_out[...] = (nn(nin, weight(w, slice(2 * width, 3 * width))) + vec[3:4, :]).astype(BF16)


def attend_kernel(meta, q_out, k_out, v_out, bias, ctx_out, lse_out, base):
    rows, width = q_out.shape
    unit = rows // UNITS
    window = rows - unit
    head = width // HEADS
    ranges = [unit_range(meta, u, unit) for u in range(UNITS)]
    column = lax.broadcasted_iota(jnp.int32, (1, window), 1)
    masks = [
        jnp.where((column + ws >= lo) & (column + ws < hi), 0.0, MASKED).astype(F32) for lo, hi, ws in ranges
    ]
    lane = lax.broadcasted_iota(jnp.int32, (unit, LANES), 1)
    lse_out[...] = jnp.zeros_like(lse_out)

    def pair(hp, carry):
        cols = pl.ds(pl.multiple_of(hp * LANES, LANES), LANES)
        for sub in range(2):
            base[sub] = skewed(bias[pl.ds(2 * hp + sub, 1), :], unit)
        for u in range(UNITS):
            ws = ranges[u][2]
            win = pl.ds(pl.multiple_of(ws, LANES), window)
            shift = pl.ds(pl.multiple_of(ws + (rows - unit) - u * unit, LANES), window)
            urows = slice(u * unit, (u + 1) * unit)
            kk = k_out[win, cols]
            vv = v_out[win, cols]
            qu = q_out[urows, cols]
            parts = []
            lses = lse_out[urows, :]
            for sub in range(2):
                qs = jnp.where((lane >= head) == bool(sub), qu, jnp.zeros_like(qu))
                s = nt(qs, kk) + (base[sub, :, shift] + masks[u])
                top = jnp.max(s, axis=1, keepdims=True)
                e = jnp.exp(s - top)
                tot = jnp.sum(e, axis=1, keepdims=True)
                parts.append(nn(e.astype(BF16), vv) * (1.0 / tot))
                lses = jnp.where(lane == 2 * hp + sub, top + jnp.log(tot), lses)
            lse_out[urows, :] = lses
            ctx_out[urows, cols] = jnp.where(lane < head, parts[0], parts[1]).astype(BF16)
        return carry

    lax.fori_loop(0, HEADS // 2, pair, 0)


def small_vectors(core, chips, parts, crossed, at, rows_d, rows_ff, vec3, inner3, table):
    half = parts[0].shape[0]
    lane = lax.broadcasted_iota(jnp.int32, (8, LANES), 1)
    vec3[...] = jnp.zeros_like(vec3)
    inner3[...] = jnp.zeros_like(inner3)
    for i, j in enumerate(crossed):
        mine = parts[i // half][i % half, :, at : at + LANES].astype(F32)
        theirs = parts[2 + j // half][j % half, :, at : at + LANES].astype(F32)
        for plane in range(2):
            block = jnp.where(core == plane, mine, theirs)
            d = 2 * chips[i] + plane
            for rows, part, out in ((rows_d, block[0:8], vec3), (rows_ff, block[8:16], inner3)):
                tile = (d * rows) >> 7
                shift = (d * rows) & (LANES - 1)
                rolled = pltpu.roll(part, shift, 1)
                out[tile] += jnp.where(lane >= shift, rolled, 0.0)
                out[tile + 1] += jnp.where(lane < shift, rolled, 0.0)
            table[pl.ds(d, 1), :] = block[9:10]


def relative_rows(bucket, table, out):
    devices = lax.broadcasted_iota(jnp.int32, (table.shape[0], bucket.shape[1]), 0)
    hot = jnp.where(devices == bucket[0:1, :], 1.0, 0.0).astype(BF16)
    rows = tn(table[...].astype(BF16), hot)
    total = jnp.zeros((HEADS, bucket.shape[1]), F32)
    for m in range(LANES // HEADS):
        total = total + jnp.where(bucket[1:2, :] == m, rows[m * HEADS : (m + 1) * HEADS], 0.0)
    out[0:HEADS, :] = total
    out[HEADS:, :] = jnp.zeros_like(out[HEADS:, :])


def project_kernel(
    meta, frames, p0, p1, p2, p3, bucket, bucket_rev,
    q_out, k_out, v_out, nin_out, w, vec, b_inner, bias, bias_rev,
    vec3, inner3, table, *, crossed, rows_d, rows_ff,
):
    width = frames.shape[1]
    core = meta[5]
    chips = [meta[6 + i] for i in range(len(crossed))]
    parts = (p0, p1, p2, p3)
    small_vectors(core, chips, parts, crossed, 3 * width, rows_d, rows_ff, vec3, inner3, table)
    for a in range(width // LANES):
        vec[:, a * LANES : (a + 1) * LANES] = vec3[a]
    for a in range(b_inner.shape[1] // LANES):
        b_inner[:, a * LANES : (a + 1) * LANES] = inner3[a, 0:1]
    relative_rows(bucket, table, bias)
    relative_rows(bucket_rev, table, bias_rev)
    unpack(core, chips, parts, crossed, w, slice(0, 3 * width))
    project_body(meta, frames, w, vec, q_out, k_out, v_out, nin_out)


def inner_kernel(meta, frames, ctx, *refs, crossed, rows_ff):
    if crossed:
        p0, p1, p2, p3, vec, b_inner, cot, att_out, nmid_out, act_out, slope_out, send, keep, w = refs
        core = meta[5]
        chips = [meta[6 + i] for i in range(len(crossed))]
        place = [meta[6 + len(crossed) + i] for i in range(2 * len(crossed))]
        unpack(core, chips, (p0, p1, p2, p3), crossed, w, slice(None))
    else:
        w, vec, b_inner, cot, att_out, nmid_out, act_out, slope_out, send, keep = refs
    width = frames.shape[1]
    ff = b_inner.shape[1]
    attended = frames[...].astype(F32) + nn(ctx[...], weight(w, slice(ff, ff + width))) + vec[4:5, :]
    att_out[...] = attended
    n, _ = normalise(attended)
    nmid_out[...] = (n * vec[5:6, :] + vec[6:7, :]).astype(BF16)
    for t in range(ff // width):
        cols = slice(t * width, (t + 1) * width)
        v = nn(nmid_out[...], weight(w, cols)) + b_inner[:, cols]
        phi = 0.5 * (1.0 + lax.erf(v * (0.5**0.5)))
        act = (v * phi).astype(BF16)
        act_out[:, cols] = act
        slope_out[:, cols] = (phi + v * jnp.exp(-0.5 * v * v) * 0.3989422804014327).astype(BF16)
        g = tn(act, cot[...])
        if crossed:
            put_blocks(core, place, t * (width // rows_ff), g, send, keep, rows_ff, slice(None))
        else:
            keep[cols, :] = g.astype(BF16)


def outer_kernel(meta, act, slope, attended, cot, *refs, crossed):
    if crossed:
        p0, p1, p2, p3, w, ctx, vec, mixed_out, gatt_out, gctx_out, gi_out, gvec_out, acc, gmid, w_outer = refs
        core = meta[5]
        chips = [meta[6 + i] for i in range(len(crossed))]
        unpack(core, chips, (p0, p1, p2, p3), crossed, w_outer, slice(None))
        w_outer = w_outer.reshape(act.shape[1], attended.shape[1])
    else:
        w_outer, w, ctx, vec, mixed_out, gatt_out, gctx_out, gi_out, gvec_out, acc, gmid = refs
    width = attended.shape[1]
    ff = act.shape[1]
    acc[...] = attended[...] + vec[7:8, :]
    gmid[...] = jnp.zeros_like(gmid)
    for t in range(ff // width):
        cols = slice(t * width, (t + 1) * width)
        wo = w_outer[cols, :]
        acc[...] += nn(act[:, cols], wo)
        gi = (slope[:, cols].astype(F32) * nt(cot[...], wo)).astype(BF16)
        gi_out[:, cols] = gi
        gmid[...] += nt(gi, weight(w, cols))
    mixed_out[...] = acc[...].astype(BF16)
    n, r = normalise(attended[...])
    e = gmid[...]
    c32 = cot[...].astype(F32)
    gatt = c32 + norm_backward(n, r, vec[5:6, :], e)
    gatt_out[...] = gatt
    gbr = gatt.astype(BF16)
    gctx_out[...] = nt(gbr, weight(w, slice(ff, ff + width))).astype(BF16)
    gvec_out[0:1, :] = jnp.sum(gbr.astype(F32), axis=0, keepdims=True)
    gvec_out[1:2, :] = jnp.sum(e * n, axis=0, keepdims=True)
    gvec_out[2:3, :] = jnp.sum(e, axis=0, keepdims=True)
    gvec_out[3:4, :] = jnp.sum(c32, axis=0, keepdims=True)
    gvec_out[4:8, :] = jnp.zeros_like(gvec_out[4:8, :])


def outer_weights_kernel(meta, nmid, gi, ctx, gatt, send, keep, gb_out, *, crossed, rows_d):
    width = nmid.shape[1]
    ff = gi.shape[1]
    core = meta[5]
    place = [meta[6 + len(crossed) + i] for i in range(2 * len(crossed))]
    for t in range(ff // width + 1):
        cols = slice(t * width, (t + 1) * width)
        if t < ff // width:
            d = gi[:, cols]
            gb_out[:, cols] = jnp.sum(d.astype(F32), axis=0, keepdims=True)
            g = tn(nmid[...], d)
        else:
            g = tn(ctx[...], gatt[...].astype(BF16))
        if crossed:
            put_blocks(core, place, 0, g, send, keep, rows_d, cols)
        else:
            keep[:, cols] = g.astype(BF16)


def small_blocks(core, place, vecs, inner, grows, bucket_rev, send, keep, columns, rows_d, rows_ff):
    n = len(place)
    span = bucket_rev.shape[1]
    row = lax.broadcasted_iota(jnp.int32, (8, LANES), 0)
    lane = lax.broadcasted_iota(jnp.int32, (8, LANES), 1)
    each = LANES // HEADS
    big = [jnp.where(bucket_rev[1:2, :] == m, grows, 0.0) for m in range(each)]
    big = jnp.concatenate(big + [jnp.zeros((LANES - each * HEADS, span), F32)], axis=0)
    high = big.astype(BF16)
    low = (big - high.astype(F32)).astype(BF16)
    hot = jnp.where(lax.broadcasted_iota(jnp.int32, (n, span), 0) == bucket_rev[0:1, :], 1.0, 0.0).astype(BF16)
    table = nt(hot, high) + nt(hot, low)

    def cut(value, at, count):
        tile, shift = at // LANES, at % LANES
        out = value[:, tile * LANES : (tile + 1) * LANES]
        if shift:
            out = pltpu.roll(out, LANES - shift, 1)
            if shift + count > LANES:
                more = pltpu.roll(value[:, (tile + 1) * LANES : (tile + 2) * LANES], LANES - shift, 1)
                out = jnp.where(lane < LANES - shift, out, more)
        return jnp.where(lane < count, out, 0.0)

    for d in range(n):
        low_rows = jnp.where(row == 0, cut(inner, d * rows_ff, rows_ff), 0.0)
        low_rows = jnp.where(row == 1, table[d : d + 1], low_rows)
        block = [cut(vecs, d * rows_d, rows_d), low_rows]
        block = jnp.concatenate(block + [jnp.zeros((rows_d - 16, LANES), F32)], axis=0).astype(BF16)
        where = place[d]

        @pl.when(core == d % 2)
        def _(block=block, where=where):
            keep[where, :, columns] = block

        @pl.when(core != d % 2)
        def _(block=block, where=where):
            send[where, :, columns] = block


def attend_back_kernel(
    meta, q, k, v, lse, ctx, gctx, bias_rev, nin, frames, gatt, gin, w, vec, *refs, crossed, rows_d, first, count,
):
    last = first + 2 * count == HEADS
    if last and crossed:
        gvec2, gb_inner, bucket_rev, *refs = refs
        earlier = first // (2 * count)
        before = [(refs[2 * i], refs[2 * i + 1]) for i in range(earlier)]
        refs = refs[2 * earlier :]
    send, keep, gin_out, gvec_out, grow_out, base, gbase, lse_t, delta_t, kt, dqkv, gk, gv = refs
    rows, width = frames.shape
    unit = rows // UNITS
    window = rows - unit
    head = width // HEADS
    core = meta[5]
    place = [meta[6 + len(crossed) + i] for i in range(2 * len(crossed))]
    lses = jnp.transpose(lse[...])
    prod = gctx[...].astype(F32) * ctx[...].astype(F32)
    sel_row = lax.broadcasted_iota(jnp.int32, (16, width), 0)
    sel_col = lax.broadcasted_iota(jnp.int32, (16, width), 1)
    sel = jnp.where((sel_col >= sel_row * head) & (sel_col < (sel_row + 1) * head), 1.0, 0.0).astype(BF16)
    high = prod.astype(BF16)
    low = (prod - high.astype(F32)).astype(BF16)
    deltas = nt(sel, high) + nt(sel, low)
    for h in range(HEADS):
        lse_t[h] = lses[h : h + 1]
        delta_t[h] = deltas[h : h + 1]
    ranges = [unit_range(meta, u, unit) for u in range(UNITS)]
    row_at = lax.broadcasted_iota(jnp.int32, (window, LANES), 0)
    lane = lax.broadcasted_iota(jnp.int32, (unit, LANES), 1)
    sub_lane = lax.broadcasted_iota(jnp.int32, (LANES, unit), 0)
    span = count * LANES

    def pair(step, carry):
        hp = first // 2 + step
        cols = pl.ds(pl.multiple_of(hp * LANES, LANES), LANES)
        here = pl.multiple_of(step * LANES, LANES)
        kt[...] = jnp.transpose(k[:, cols])
        gk[...] = jnp.zeros_like(gk)
        gv[...] = jnp.zeros_like(gv)
        gbase[...] = jnp.zeros_like(gbase)
        for sub in range(2):
            base[sub] = skewed(bias_rev[pl.ds(2 * hp + sub, 1), :], unit)
        for u in range(UNITS):
            lo, hi, ws = ranges[u]
            ws = pl.multiple_of(ws, LANES)
            win = pl.ds(ws, window)
            urows = slice(u * unit, (u + 1) * unit)
            mask = jnp.where((row_at + ws >= lo) & (row_at + ws < hi), 0.0, MASKED).astype(F32)
            kk = k[win, cols]
            vv = v[win, cols]
            qu = q[urows, cols]
            gu = gctx[urows, cols]
            gk_win = gk[win, :]
            gv_win = gv[win, :]
            gq = []
            offsets = [
                pl.ds(pl.multiple_of((rows - unit) + u * unit - ws - jb * unit, LANES), unit) for jb in range(UNITS - 1)
            ]
            for sub in range(2):
                h = 2 * hp + sub
                mine = (lane >= head) == bool(sub)
                qs = jnp.where(mine, qu, jnp.zeros_like(qu))
                gs = jnp.where(mine, gu, jnp.zeros_like(gu))
                rel = jnp.concatenate([base[sub, :, o] for o in offsets], axis=0)
                s = nt(kk, qs) + rel + mask
                p = jnp.exp(s - lse_t[h, :, urows])
                gp = nt(vv, gs)
                ds = (p * (gp - delta_t[h, :, urows])).astype(BF16)
                gv_win = gv_win + nn(p.astype(BF16), gs)
                gk_win = gk_win + nn(ds, qs)
                gq.append(nn(kt[:, win], ds))
                d32 = ds.astype(F32)
                for jb, o in enumerate(offsets):
                    gbase[sub, :, o] += d32[jb * unit : (jb + 1) * unit]
            gk[win, :] = gk_win
            gv[win, :] = gv_win
            gq_t = jnp.where(sub_lane < head, gq[0], gq[1])
            dqkv[urows, pl.ds(here, LANES)] = jnp.transpose(gq_t).astype(BF16) * BF16(head**-0.5)
        dqkv[:, pl.ds(span + here, LANES)] = gk[...].astype(BF16)
        dqkv[:, pl.ds(2 * span + here, LANES)] = gv[...].astype(BF16)
        for sub in range(2):
            grow_out[pl.ds(2 * step + sub, 1), :] = unskewed_sum(gbase[sub], unit)
        return carry

    grow_out[...] = jnp.zeros_like(grow_out)
    lax.fori_loop(0, count, pair, 0)
    at_columns = first * head
    grad_in = gin[...] if first else jnp.zeros((rows, width), F32)
    for part in range(3):
        d = dqkv[:, part * span : (part + 1) * span]
        grad_in = grad_in + nt(d, weight(w, slice(part * width + at_columns, part * width + at_columns + span)))
    g = tn(nin[...], dqkv[...])
    if crossed:
        put_blocks(core, place, 0, g, send, keep, rows_d, slice(0, 3 * span))
    else:
        keep[:, 0 : 3 * span] = g.astype(BF16)
    sums = [jnp.sum(dqkv[:, at : at + span].astype(F32), axis=0, keepdims=True) for at in (0, 2 * span)]
    gvec_out[...] = jnp.zeros_like(gvec_out)
    gvec_out[2:4, 0:span] = jnp.concatenate(sums, axis=0)
    if not last:
        gin_out[...] = grad_in
        return
    n, r = normalise(frames[...].astype(F32))
    gin_out[...] = (gatt[...] + norm_backward(n, r, vec[0:1, :], grad_in)).astype(BF16)
    gvec_out[0:1, :] = jnp.sum(grad_in * n, axis=0, keepdims=True)
    gvec_out[1:2, :] = jnp.sum(grad_in, axis=0, keepdims=True)
    if crossed:
        for i, (vectors, _) in enumerate(before):
            gvec_out[2:4, i * span : (i + 1) * span] = vectors[2:4, 0:span]
        gvec_out[2:4, at_columns : at_columns + span] = jnp.concatenate(sums, axis=0)
        gvec_out[4:8, :] = gvec2[0:4, :]
        grows = jnp.concatenate([grow[0 : 2 * count, :] for _, grow in before] + [grow_out[0 : 2 * count, :]], axis=0)
        small_blocks(
            core, place, gvec_out[...], jnp.broadcast_to(gb_inner[...], (8, gb_inner.shape[1])), grows, bucket_rev,
            send, keep, slice(3 * span, 3 * span + LANES), rows_d, gb_inner.shape[1] // len(place),
        )


def run_kernel(order, kernel, name, scalars, arrays, outs, scratch=(), spare=10):
    spec = pl.BlockSpec(memory_space=pltpu.VMEM)
    smem = pl.BlockSpec(memory_space=pltpu.SMEM)
    arrays = order.after(*arrays)
    arrays = [pltpu.with_memory_space_constraint(a, pltpu.VMEM) for a in arrays]
    limit = spare * MIB + sum(math.prod(b.shape) * jnp.dtype(b.dtype).itemsize for b in scratch)
    out = pl.pallas_call(
        kernel,
        in_specs=[smem] * len(scalars) + [spec] * len(arrays),
        out_specs=[spec] * len(outs),
        out_shape=[pltpu.VMEM(s, d) for s, d in outs],
        scratch_shapes=list(scratch),
        compiler_params=pltpu.CompilerParams(vmem_limit_bytes=limit),
        cost_estimate=pl.CostEstimate(flops=100_000_000_000, bytes_accessed=100_000_000, transcendentals=0),
        name=name,
    )(*scalars, *arrays)
    order.did(out[0])
    return out


def on_device(
    frames, ln1_gain, ln1_shift, w_query, b_query, w_key, w_value, b_value, w_out, b_out, ln2_gain, ln2_shift,
    w_inner, b_inner, w_outer, b_outer, bias_table, layout, valid, rel_index, cotangent, *, n,
):
    rows, width = frames.shape
    rows_d = w_query.shape[0]
    rows_ff = w_outer.shape[0]
    ff = w_inner.shape[1]
    span = rel_index.shape[0] + 1
    unit = rows // UNITS
    per_table = bias_table.shape[0]
    plan = plan_tables(n)
    core, chips, place = plan
    order = Order()
    direct = (
        rows_d % 8 == 0 and rows_ff % 16 == 0 and max(rows_d, rows_ff, per_table) <= LANES and per_table % HEADS == 0
    )
    crossed = tuple(crossed_places(n)) if direct else ()
    meta = jnp.concatenate([layout, valid.reshape(-1), core[None]] + [chips, place] * direct).astype(jnp.int32)
    small_d = jnp.stack([ln1_gain, ln1_shift, b_query, b_value, b_out, ln2_gain, ln2_shift, b_outer])

    base = pltpu.VMEM((2, unit, span), F32)
    if direct:
        wide = [jnp.pad(small_d, ((0, 0), (0, LANES - rows_d))), jnp.pad(b_inner, (0, LANES - rows_ff))[None]]
        wide.append(jnp.pad(bias_table, (0, LANES - per_table))[None])
        small = jnp.pad(jnp.concatenate(wide), ((0, rows_d - 10), (0, 0)))
        g1 = Gather(jnp.concatenate([w_query, w_key, w_value, small], axis=1), n, order)
        (part2,) = lax.optimization_barrier((jnp.concatenate([w_inner, w_out], axis=1), g1.got))[:1]
        g2 = Gather(part2, n, order)
        (part3,) = lax.optimization_barrier((w_outer, g2.got))[:1]
        g3 = Gather(part3, n, order)
        for g in (g1, g1, g2, g1, g2, g3, g2):
            g.step()
        first = g1.finish()
        each = per_table // HEADS
        index = jnp.stack([rel_index // each, rel_index % each])
        bucket = jnp.pad(index, ((0, 6), (0, 1)), constant_values=-1)
        bucket_rev = jnp.pad(index[:, ::-1], ((0, 6), (0, 1)), constant_values=-1)
        q, k, v, nin, w1, vec, inner_bias, bias, bias_rev = run_kernel(
            order, functools.partial(project_kernel, crossed=crossed, rows_d=rows_d, rows_ff=rows_ff), "project", [meta],
            [frames, *first, bucket, bucket_rev],
            [((rows, width), BF16)] * 4
            + [((n // 2, 2 * rows_d, 3 * width), BF16), ((8, width), F32), ((1, ff), F32), ((16, span), F32), ((16, span), F32)],
            [
                pltpu.VMEM((width // LANES + 1, 8, LANES), F32),
                pltpu.VMEM((ff // LANES + 1, 8, LANES), F32),
                pltpu.VMEM((n, LANES), F32),
            ],
        )
        g3.step()
        w2 = g2.finish()
        part_ff = [((n // 2, rows_ff, width), BF16)] * 2
        part_io = [((n // 2, rows_d, ff + width), BF16)] * 2
        w2_out = [((n // 2, 2 * rows_d, ff + width), BF16)]
    else:
        flat = jnp.concatenate([small_d.reshape(-1), b_inner, bias_table])
        per = flat.shape[0] // rows_d
        small = jnp.pad(flat.reshape(rows_d, per), ((0, 0), (0, LANES - per)))
        w1 = gathered(Gather(jnp.concatenate([w_query, w_key, w_value, small], axis=1), n, order).finish(), plan, n)
        w2 = (gathered(Gather(jnp.concatenate([w_inner, w_out], axis=1), n, order).finish(), plan, n),)
        w3 = (gathered(Gather(w_outer, n, order).finish(), plan, n),)
        flats = w1[:, 3 * width : 3 * width + per].reshape(n, rows_d * per)
        vec = flats[:, : 8 * rows_d].reshape(n, 8, rows_d).transpose(1, 0, 2).reshape(8, width).astype(F32)
        inner_bias = flats[:, 8 * rows_d : 8 * rows_d + rows_ff].reshape(1, ff).astype(F32)
        table = jnp.pad(flats[:, 8 * rows_d + rows_ff :].reshape(-1, HEADS), ((0, 0), (0, 16 - HEADS)))
        index = jnp.pad(rel_index, (0, 1), constant_values=-1)
        index_rev = jnp.pad(rel_index[::-1], (0, 1), constant_values=-1)
        ids = jnp.arange(table.shape[0], dtype=jnp.int32)[:, None]
        bias = tn(table, (ids == index[None]).astype(BF16))
        bias_rev = tn(table, (ids == index_rev[None]).astype(BF16))
        q, k, v, nin = run_kernel(
            order, project_body, "project", [meta], [frames, w1, vec], [((rows, width), BF16)] * 4
        )
        part_ff = [((8, LANES), BF16), ((ff, width), BF16)]
        part_io = [((8, LANES), BF16), ((width, ff + width), BF16)]
        w2_out = []

    ctx, lse = run_kernel(
        order, attend_kernel, "attend", [meta], [q, k, v, bias], [((rows, width), BF16), ((rows, LANES), F32)], [base]
    )

    def start(send, keep, scatter=None):
        scatter = scatter or Scatter(n, order)
        return scatter.add(*((send, keep) if direct else split_natural(keep, plan, n)))

    if direct:
        g3.step()
    attended, nmid, act, slope, ff_send, ff_keep, *w2_whole = run_kernel(
        order, functools.partial(inner_kernel, crossed=crossed, rows_ff=rows_ff), "inner", [meta],
        [frames, ctx, *w2, vec, inner_bias, cotangent],
        [((rows, width), F32), ((rows, width), BF16), ((rows, ff), BF16), ((rows, ff), BF16)] + part_ff + w2_out,
    )
    w2_whole = w2_whole[0] if direct else w2[0]
    sum_ff = start(ff_send, ff_keep)
    if direct:
        w3 = g3.finish()
    mixed, gatt, gctx, gi, gvec2 = run_kernel(
        order, functools.partial(outer_kernel, crossed=crossed), "outer", [meta],
        [act, slope, attended, cotangent, *w3, w2_whole, ctx, vec],
        [((rows, width), BF16), ((rows, width), F32), ((rows, width), BF16), ((rows, ff), BF16), ((8, width), F32)],
        [pltpu.VMEM((rows, width), F32)] * 2 + [pltpu.VMEM((n // 2, 2 * rows_ff, width), BF16)] * direct,
    )
    sum_ff.step()
    io_send, io_keep, gb_inner = run_kernel(
        order, functools.partial(outer_weights_kernel, crossed=crossed, rows_d=rows_d), "outer_weights", [meta],
        [nmid, gi, ctx, gatt], part_io + [((1, ff), F32)],
    )
    sum_io = start(io_send, io_keep)

    count = 2
    cols = count * LANES
    passed = gatt
    done, earlier = [], []
    begin = functools.partial(Scatter, n, order)
    sum_early, sum_late = begin(), begin()
    calls = HEADS // (2 * count)
    for call in range(calls):
        last = call == calls - 1
        wide = 3 * cols + LANES * (last and direct)
        part = [((n // 2, rows_d, wide), BF16)] * 2 if direct else [((8, LANES), BF16), ((width, wide), BF16)]
        extra = [gvec2, gb_inner, bucket_rev] + [a for pair in earlier for a in pair] if last and direct else []
        send, keep, passed, gvec1, grow = run_kernel(
            order,
            functools.partial(
                attend_back_kernel, crossed=crossed, rows_d=rows_d, first=call * 2 * count, count=count
            ),
            "attend_back", [meta],
            [q, k, v, lse, ctx, gctx, bias_rev, nin, frames, gatt, passed, w1, vec] + extra,
            part + [((rows, width), BF16 if last else F32), ((8, width), F32), ((8, span), F32)],
            [
                base, base,
                pltpu.VMEM((HEADS, 1, rows), F32),
                pltpu.VMEM((HEADS, 1, rows), F32),
                pltpu.VMEM((LANES, rows), BF16),
                pltpu.VMEM((rows, 3 * cols), BF16),
                pltpu.VMEM((rows, LANES), F32),
                pltpu.VMEM((rows, LANES), F32),
            ],
            spare=10,
        )
        earlier.append((gvec1, grow))
        start(send, keep, sum_late if last else sum_early)
        if call == 0:
            sum_ff.step()
            sum_io.step()
        if call == 1:
            sum_ff.step()
            sum_early.step()
    tail = [sum_io, sum_ff, sum_early, sum_late, sum_io, sum_early, sum_late, sum_io, sum_early, sum_late, sum_late]
    for each_sum in tail:
        if each_sum.steps:
            each_sum.step()
    sum_outer = sum_ff.finish()
    early, sum_io, late = sum_early.finish(), sum_io.finish(), sum_late.finish()
    pieces = [early[:, i * 3 * cols : (i + 1) * 3 * cols] for i in range(calls - 1)] + [late[:, : 3 * cols]]
    sum_q, sum_k, sum_v = (jnp.concatenate([p[:, i * cols : (i + 1) * cols] for p in pieces], axis=1) for i in range(3))
    if direct:
        small = late[:, 3 * cols :]
        vecs = small[:8, :rows_d]
        sum_b_inner = small[8, :rows_ff]
        sum_table = small[9, :per_table]
    else:
        hot_rev = (ids == index_rev[None]).astype(F32)
        grow = jnp.concatenate([g[: 2 * count] for _, g in earlier])
        gtable = lax.dot_general(
            hot_rev, grow, (((1,), (1,)), ((), ())), precision=lax.Precision.HIGHEST, preferred_element_type=F32
        )
        gbias = jnp.concatenate([g[2:4, :cols] for g, _ in earlier], axis=1)
        gsmall = jnp.concatenate([gvec1[0:2], gbias, gvec2[0:4]])
        gsmall = gsmall.reshape(8, n, rows_d).transpose(1, 0, 2).reshape(n, 8 * rows_d)
        gflat = jnp.concatenate([gsmall, gb_inner.reshape(n, rows_ff), gtable.reshape(n, -1)], axis=1)
        gflat = jnp.pad(gflat, ((0, 0), (0, -gflat.shape[1] % LANES))).astype(BF16)
        sum_flat = Scatter(n, order).add(*split_natural(gflat, plan, n)).finish()[0]
        vecs = sum_flat[: 8 * rows_d].reshape(8, rows_d)
        sum_b_inner = sum_flat[8 * rows_d : 8 * rows_d + rows_ff]
        sum_table = sum_flat[8 * rows_d + rows_ff : 8 * rows_d + rows_ff + per_table]
    return (
        mixed, passed, vecs[0], vecs[1], sum_q, vecs[2], sum_k, sum_v, vecs[3],
        sum_io[:, ff:], vecs[4], vecs[5], vecs[6], sum_io[:, :ff], sum_b_inner, sum_outer, vecs[7], sum_table,
    )


def solution(mesh):
    row, two = P("dp"), P("dp", None)
    in_specs = (two, row, row, two, row, two, two, row, two, row, row, row, two, row, two, row, row, row, two, P(), two)
    out_specs = (two, two, row, row, two, row, two, two, row, two, row, row, row, two, row, two, row, row)
    return jax.shard_map(
        functools.partial(on_device, n=mesh.shape["dp"]),
        mesh=mesh, in_specs=in_specs, out_specs=out_specs, check_vma=False,
    )
```

time: 339 us -> 257 us (0.76)
  Pallas kernels: 120 us -> 88.3 us
  waiting for transfers between devices: 125 us -> 102 us
  other arithmetic: 22.9 us -> 13.4 us
  starting transfers between devices: 46.3 us -> 36.9 us
  local copies, waits for them, and re-layouts: 19.2 us -> 12.7 us
  matrix products: 3.42 us -> 0 us
    pallas_call x3 -> x0, Pallas kernels: 29.2 us -> none  [assemble(): pl.pallas_call(functools.partial(assemble_kernel, half=half), grid_spec=p...]
    ppermute x38 -> x39, waiting for transfers between devices: 125 us -> 102 us  [the longest x9 49.2 us: step(): self.got = lax.ppermute(self.held, 'dp', pairs(self.n, self.steps.pop(0)))]
    slice x11 -> x2, local copies, waits for them, and re-layouts: 11.8 us -> 0.02 us  [on_device(): p[:, i * cols:(i + 1) * cols]]
    ppermute x38 -> x39, starting transfers between devices: 46.3 us -> 36.9 us  [the longest x16 14.8 us: step(): lax.ppermute(out, 'dp', pairs(self.n, by_core))]
    unnamed x26 -> x54, local copies, waits for them, and re-layouts: 0.21 us -> 6.12 us
    convert_element_type x18 -> x15, other arithmetic: 11.3 us -> 6.47 us  [total(): out = out.astype(dtype)]
    dot_general x3 -> x0, matrix products: 3.42 us -> none  [the longest x2 1.91 us: tn(): lax.dot_general(a, b, (((0,), (0,)), ((), ())), preferred_element_type=F32)]
    pallas_call x4 -> x8, Pallas kernels: 90.6 us -> 88.3 us  [run_kernel(): pl.pallas_call(kernel, in_specs=[smem] * len(scalars) + [spec] * len(arra...]
  transfers between devices with their start and end apart: 38 -> 39, of which waited for: 20 -> 21; matrix products, arithmetic and copies ran while one was open for 11% -> 6% of each run, Pallas kernels for 27% -> 35%
where the time goes in v2:
time: 257 us; the launch traced here: 255 us
  waiting for transfers between devices  102 us (40%)
  Pallas kernels  88.3 us (34%)
  starting transfers between devices  36.9 us (14%)
  other arithmetic  13.4 us (5%)
  local copies, waits for them, and re-layouts  12.7 us (5%)
    pallas_call x8, Pallas kernels, run_kernel(): pl.pallas_call(kernel, in_specs=[smem] * len(scalars) + [spec] * len(arra...  88.3 us
    ppermute x9, waiting for transfers between devices, step(): self.got = lax.ppermute(self.held, 'dp', pairs(self.n, self.steps.pop(0)))  49.2 us
    ppermute x16, waiting for transfers between devices, step(): lax.ppermute(out, 'dp', pairs(self.n, by_core))  39.3 us
    ppermute x16, starting transfers between devices, step(): lax.ppermute(out, 'dp', pairs(self.n, by_core))  14.8 us
    ppermute x3, waiting for transfers between devices, __init__(): self.got = lax.ppermute(self.held, 'dp', pairs(n, self.steps.pop(0)))  13.3 us
    ppermute x3, starting transfers between devices, __init__(): self.got = lax.ppermute(self.held, 'dp', pairs(n, self.steps.pop(0)))  10.6 us
    ppermute x9, starting transfers between devices, step(): self.got = lax.ppermute(self.held, 'dp', pairs(self.n, self.steps.pop(0)))  9.52 us
    convert_element_type x15, other arithmetic, total(): out = out.astype(dtype)  6.47 us
  transfers between devices with their start and end apart: 39, of which 21 were waited for; matrix products, arithmetic and copies ran while one was open for 6% of the time, Pallas kernels for 35%

profile of v2, /device:TPU:0, one launch (start us, length us, event | category | flops | bytes accessed | tf_op | source)
XLA Modules:
  0.0 255.5 jit_solution(6281006435366547967)
XLA Ops:
  3.0 4.1 %collective-permute-start = (bf16[1,24,2432]{2,1,0:T(8,128)(2,1)S(1)}, bf16[1,24,2432]{2,1,0:T(8,128)(2,1)S(1)}, u32[]{:S(2)}, u32[]{:S(2)}) collective-permute-start(bf16[1,24,2432]{2,1,0:T(8,128)(2,1)S(1)} %fusion.11), channel_id=1, source_target_pairs={{0,16},{1,17},{2,18},{3,19},{4,20},{5,21},{6,22},{7,23},{8,24},{9,... | collective-permute-start | bytes 350216 | tf_op jit(solution)/shard_map/ppermute | solution.py:66
  7.1 5.7 %collective-permute-done = bf16[1,24,2432]{2,1,0:T(8,128)(2,1)S(1)} collective-permute-done((bf16[1,24,2432]{2,1,0:T(8,128)(2,1)S(1)}, bf16[1,24,2432]{2,1,0:T(8,128)(2,1)S(1)}, u32[]{:S(2)}, u32[]{:S(2)}) %collective-permute-start) | collective-permute-done | bytes 116768 | tf_op jit(solution)/shard_map/ppermute | solution.py:66
  15.2 3.4 %collective-permute-start.3 = (bf16[1,24,3840]{2,1,0:T(8,128)(2,1)S(1)}, bf16[1,24,3840]{2,1,0:T(8,128)(2,1)S(1)}, u32[]{:S(2)}, u32[]{:S(2)}) collective-permute-start(bf16[1,24,3840]{2,1,0:T(8,128)(2,1)S(1)} %bitcast.48), channel_id=1, source_target_pairs={{0,16},{1,17},{2,18},{3,19},{4,20},{5,21},{6,22},{7,23},{8,24},{9,... | collective-permute-start | bytes 552968 | tf_op jit(solution)/shard_map/ppermute | solution.py:66
  18.7 3.8 %collective-permute-done.1 = bf16[2,24,2432]{2,1,0:T(8,128)(2,1)S(1)} collective-permute-done((bf16[2,24,2432]{2,1,0:T(8,128)(2,1)S(1)}, bf16[2,24,2432]{2,1,0:T(8,128)(2,1)S(1)}, u32[]{:S(2)}, u32[]{:S(2)}) %collective-permute-start.1) | collective-permute-done | bytes 233504 | tf_op jit(solution)/shard_map/ppermute | solution.py:72
  23.6 3.6 %collective-permute-done.3 = bf16[1,24,3840]{2,1,0:T(8,128)(2,1)S(1)} collective-permute-done((bf16[1,24,3840]{2,1,0:T(8,128)(2,1)S(1)}, bf16[1,24,3840]{2,1,0:T(8,128)(2,1)S(1)}, u32[]{:S(2)}, u32[]{:S(2)}) %collective-permute-start.3) | collective-permute-done | bytes 184352 | tf_op jit(solution)/shard_map/ppermute | solution.py:66
  27.3 6.0 %collective-permute-done.2 = bf16[4,24,2432]{2,1,0:T(8,128)(2,1)S(1)} collective-permute-done((bf16[4,24,2432]{2,1,0:T(8,128)(2,1)S(1)}, bf16[4,24,2432]{2,1,0:T(8,128)(2,1)S(1)}, u32[]{:S(2)}, u32[]{:S(2)}) %collective-permute-start.2) | collective-permute-done | bytes 466976 | tf_op jit(solution)/shard_map/ppermute | solution.py:72
  41.7 4.0 %collective-permute-done.9 = bf16[1,96,768]{2,1,0:T(8,128)(2,1)} collective-permute-done((bf16[1,96,768]{2,1,0:T(8,128)(2,1)}, bf16[1,96,768]{2,1,0:T(8,128)(2,1)}, u32[]{:S(2)}, u32[]{:S(2)}) %collective-permute-start.9) | collective-permute-done | bytes 147488 | tf_op jit(solution)/shard_map/ppermute | solution.py:66
  49.1 4.2 %collective-permute-done.4.p1 = bf16[8,24,2432]{2,1,0:T(8,128)(2,1)S(1)} collective-permute-done((bf16[8,24,2432]{2,1,0:T(8,128)(2,1)S(1)}, bf16[8,24,2432]{2,1,0:T(8,128)(2,1)S(1)}, u32[]{:S(2)}, u32[]{:S(2)}) %collective-permute-start.4) | collective-permute-done | bytes 933920 | tf_op jit(solution)/shard_map/ppermute | solution.py:72
  57.1 3.8 %project.1 = (bf16[512,768]{1,0:T(8,128)(2,1)S(1)}, bf16[512,768]{1,0:T(8,128)(2,1)S(1)}, bf16[512,768]{1,0:T(8,128)(2,1)S(1)}, bf16[512,768]{1,0:T(8,128)(2,1)S...) custom-call(s32[54]{0:T(128)S(1)} %concatenate.64.meta, ...), custom_call_target="tpu_custom_call" | custom-call | flops 99999997952 | bytes 100000000 | tf_op jit(solution)/shard_map/project/pallas_call | solution.py:606
  62.6 18.9 %collective-permute-done.11.refs_1_ = bf16[8,24,3840]{2,1,0:T(8,128)(2,1)S(1)} collective-permute-done((bf16[8,24,3840]{2,1,0:T(8,128)(2,1)}, bf16[8,24,3840]{2,1,0:T(8,128)(2,1)S(1)}, u32[]{:S(2)}, u32[]{:S(2)}) %collective-permute-start.11) | collective-permute-done | bytes 1474592 | tf_op jit(solution)/shard_map/ppermute | solution.py:72
  81.5 14.1 %attend.1 = (bf16[512,768]{1,0:T(8,128)(2,1)S(1)}, f32[512,128]{1,0:T(8,128)S(1)}) custom-call(s32[54]{0:T(128)S(1)} %concatenate.64.meta, bf16[512,768]{1,0:T(8,128)(2,1)S(1)} %get-tuple-element.376.q_out.q, bf16[512,768]{1,0:T(8,128)(2,1)S(1)} %get-tuple-element.377.k_out.k, bf16[512,768]{1,0:T(8,128)(2,1)S(1)} %get-tuple-element.378.v_out.v, ...), custom_call_target="tpu_custom_call" | custom-call | flops 99999997952 | bytes 100000000 | tf_op jit(solution)/shard_map/attend/pallas_call | solution.py:606
  97.5 14.5 %collective-permute-done.15.refs_1_ = bf16[8,96,768]{2,1,0:T(8,128)(2,1)S(1)} collective-permute-done((bf16[8,96,768]{2,1,0:T(8,128)(2,1)S(1)}, bf16[8,96,768]{2,1,0:T(8,128)(2,1)S(1)}, u32[]{:S(2)}, u32[]{:S(2)}) %collective-permute-start.15) | collective-permute-done | bytes 1179680 | tf_op jit(solution)/shard_map/ppermute | solution.py:72
  112.0 24.6 %inner.1 = (f32[512,768]{1,0:T(8,128)S(1)}, bf16[512,768]{1,0:T(8,128)(2,1)S(1)}, bf16[512,3072]{1,0:T(8,128)(2,1)S(1)}, bf16[512,3072]{1,0:T(8,128)(2,1)S(1)}, ...) custom-call(s32[54]{0:T(128)S(1)} %concatenate.64.meta, ...), custom_call_target="tpu_custom_call" | custom-call | flops 99999997952 | bytes 100000000 | tf_op jit(solution)/shard_map/inner/pallas_call | solution.py:606
  137.2 10.3 %outer.1 = (bf16[512,768]{1,0:T(8,128)(2,1)S(1)}, f32[512,768]{1,0:T(8,128)S(1)}, bf16[512,768]{1,0:T(8,128)(2,1)S(1)}, bf16[512,3072]{1,0:T(8,128)(2,1)S(1)}, f32[8,768]{1,0:T(8,128)S(1)}) custom-call(s32[54]{0:T(128)S(1)} %concatenate.64.meta, bf16[512,3072]{1,0:T(8,128)(2,1)S(1)} %get-tuple-element.295.act, ...), custom_call_target="tpu_custom_call" | custom-call | flops 99999997952 | bytes 100000000 | tf_op jit(solution)/shard_map/outer/pallas_call | solution.py:606
  150.9 7.4 %outer_weights.1 = (bf16[16,24,3840]{2,1,0:T(8,128)(2,1)S(1)}, bf16[16,24,3840]{2,1,0:T(8,128)(2,1)S(1)}, f32[1,3072]{1,0:T(1,128)S(1)}) custom-call(s32[54]{0:T(128)S(1)} %concatenate.64.meta, bf16[512,768]{1,0:T(8,128)(2,1)S(1)} %get-tuple-element.319.nmid, bf16[512,3072]{1,0:T(8,128)(2,1)S(1)} %get-tuple-element.320.gi, ...), custom_call_target="tpu_custom_call" | custom-call | flops 99999997952 | bytes 100000000 | tf_op jit(solution)/shard_map/outer_weights/pallas_call | solution.py:606
  158.5 8.0 %attend_back.3 = (bf16[16,24,768]{2,1,0:T(8,128)(2,1)S(1)}, bf16[16,24,768]{2,1,0:T(8,128)(2,1)S(1)}, f32[512,768]{1,0:T(8,128)S(1)}, f32[8,768]{1,0:T(8,128)S(1)}, f32[8,1024]{1,0:T(8,128)S(1)}) custom-call(s32[54]{0:T(128)S(1)} %concatenate.64.meta, bf16[512,768]{1,0:T(8,128)(2,1)S(1)} %copy-done.8, bf16[512,768]{1,0:T(8,128)(2,1)S(1)} %copy-done.10, ...), custom_call_target="tpu_custom_call" | custom-call | flops 99999997952 | bytes 100000000 | tf_op jit(solution)/shard_map/attend_back/pallas_call | solution.py:606
  171.5 8.1 %attend_back.4 = (bf16[16,24,768]{2,1,0:T(8,128)(2,1)S(1)}, bf16[16,24,768]{2,1,0:T(8,128)(2,1)S(1)}, f32[512,768]{1,0:T(8,128)S(1)}, f32[8,768]{1,0:T(8,128)S(1)}, f32[8,1024]{1,0:T(8,128)S(1)}) custom-call(s32[54]{0:T(128)S(1)} %concatenate.64.meta, bf16[512,768]{1,0:T(8,128)(2,1)S(1)} %copy-done.8, bf16[512,768]{1,0:T(8,128)(2,1)S(1)} %copy-done.10, ...), custom_call_target="tpu_custom_call" | custom-call | flops 99999997952 | bytes 100000000 | tf_op jit(solution)/shard_map/attend_back/pallas_call | solution.py:606
  183.2 12.1 %attend_back.5 = (bf16[16,24,896]{2,1,0:T(8,128)(2,1)S(1)}, bf16[16,24,896]{2,1,0:T(8,128)(2,1)S(1)}, bf16[512,768]{1,0:T(8,128)(2,1)S(1)}, f32[8,768]{1,0:T(8,128)}, f32[8,1024]{1,0:T(8,128)}) custom-call(s32[54]{0:T(128)S(1)} %concatenate.64.meta, bf16[512,768]{1,0:T(8,128)(2,1)S(1)} %copy-done.8, bf16[512,768]{1,0:T(8,128)(2,1)S(1)} %copy-done.10, ...), custom_call_target="tpu_custom_call" | custom-call | flops 99999997952 | bytes 100000000 | tf_op jit(solution)/shard_map/attend_back/pallas_call | solution.py:606
  195.3 3.7 %collective-permute-done.27 = bf16[8,24,3840]{2,1,0:T(8,128)(2,1)S(1)} collective-permute-done((bf16[8,24,3840]{2,1,0:T(8,128)(2,1)S(1)}, bf16[8,24,3840]{2,1,0:T(8,128)(2,1)S(1)}, u32[]{:S(2)}, u32[]{:S(2)}) %collective-permute-start.27) | collective-permute-done | bytes 1474592 | tf_op jit(solution)/shard_map/ppermute | solution.py:113
  201.0 8.1 %collective-permute-done.25 = bf16[8,24,1536]{2,1,0:T(8,128)(2,1)S(1)} collective-permute-done((bf16[8,24,1536]{2,1,0:T(8,128)(2,1)S(1)}, bf16[8,24,1536]{2,1,0:T(8,128)(2,1)S(1)}, u32[]{:S(2)}, u32[]{:S(2)}) %collective-permute-start.25) | collective-permute-done | bytes 589856 | tf_op jit(solution)/shard_map/ppermute | solution.py:113
  211.5 4.0 %collective-permute-done.30 = bf16[4,24,3840]{2,1,0:T(8,128)(2,1)S(1)} collective-permute-done((bf16[4,24,3840]{2,1,0:T(8,128)(2,1)S(1)}, bf16[4,24,3840]{2,1,0:T(8,128)(2,1)S(1)}, u32[]{:S(2)}, u32[]{:S(2)}) %collective-permute-start.30) | collective-permute-done | bytes 737312 | tf_op jit(solution)/shard_map/ppermute | solution.py:113
  215.8 3.8 %collective-permute-done.29 = bf16[4,24,1536]{2,1,0:T(8,128)(2,1)S(1)} collective-permute-done((bf16[4,24,1536]{2,1,0:T(8,128)(2,1)S(1)}, bf16[4,24,1536]{2,1,0:T(8,128)(2,1)S(1)}, u32[]{:S(2)}, u32[]{:S(2)}) %collective-permute-start.29) | collective-permute-done | bytes 294944 | tf_op jit(solution)/shard_map/ppermute | solution.py:113
  220.8 5.0 %collective-permute-done.33 = bf16[2,24,3840]{2,1,0:T(8,128)(2,1)S(1)} collective-permute-done((bf16[2,24,3840]{2,1,0:T(8,128)(2,1)S(1)}, bf16[2,24,3840]{2,1,0:T(8,128)(2,1)S(1)}, u32[]{:S(2)}, u32[]{:S(2)}) %collective-permute-start.33) | collective-permute-done | bytes 368672 | tf_op jit(solution)/shard_map/ppermute | solution.py:113
  235.5 9.6 %collective-permute-done.38 = bf16[1,96,768]{2,1,0:T(8,128)(2,1)S(1)} collective-permute-done((bf16[1,96,768]{2,1,0:T(8,128)(2,1)S(1)}, bf16[1,96,768]{2,1,0:T(8,128)(2,1)S(1)}, u32[]{:S(2)}, u32[]{:S(2)}) %collective-permute-start.38) | collective-permute-done | bytes 147488 | tf_op jit(solution)/shard_map/ppermute | solution.py:113
  (178 shorter events, 62.6 us)
Async XLA Ops:
  15.2 12.0 %collective-permute-start.3 = (bf16[1,24,3840]{2,1,0:T(8,128)(2,1)S(1)}, bf16[1,24,3840]{2,1,0:T(8,128)(2,1)S(1)}, u32[]{:S(2)}, u32[]{:S(2)}) collective-permute-start(bf16[1,24,3840]{2,1,0:T(8,128)(2,1)S(1)} %bitcast.48), channel_id=1, source_target_pairs={{0,16},{1,17},{2,18},{3,19},{4,20},{5,21},{6,22},{7,23},{8,24},{9,... | collective-permute-start | bytes 552968 | tf_op jit(solution)/shard_map/ppermute | solution.py:66
  33.4 19.8 %collective-permute-start.4 = (bf16[8,24,2432]{2,1,0:T(8,128)(2,1)S(1)}, bf16[8,24,2432]{2,1,0:T(8,128)(2,1)S(1)}, u32[]{:S(2)}, u32[]{:S(2)}) collective-permute-start(bf16[8,24,2432]{2,1,0:T(8,128)(2,1)S(1)} %constant_dynamic-update-slice_fusion.4.p0), channel_id=1, source_target_pairs={{0,4},{1,3},{2,6},{3,1},{4,0},{5,7},{6,2},{7,5},{8,12},{9,11},{10,... | collective-permute-start | bytes 2801672 | tf_op jit(solution)/shard_map/ppermute | solution.py:72
  35.3 13.8 %collective-permute-start.8 = (bf16[4,24,3840]{2,1,0:T(8,128)(2,1)S(1)}, bf16[4,24,3840]{2,1,0:T(8,128)(2,1)S(1)}, u32[]{:S(2)}, u32[]{:S(2)}) collective-permute-start(bf16[4,24,3840]{2,1,0:T(8,128)(2,1)S(1)} %constant_dynamic-update-slice_fusion.6), channel_id=1, source_target_pairs={{0,2},{1,5},{2,0},{3,7},{4,6},{5,1},{6,4},{7,3},{8,10},{9,13},{10,... | collective-permute-start | bytes 2211848 | tf_op jit(solution)/shard_map/ppermute | solution.py:72
  41.7 15.4 %collective-permute-start.5 = (bf16[8,24,2432]{2,1,0:T(8,128)(2,1)S(1)}, bf16[8,24,2432]{2,1,0:T(8,128)(2,1)S(1)}, u32[]{:S(2)}, u32[]{:S(2)}) collective-permute-start(bf16[8,24,2432]{2,1,0:T(8,128)(2,1)S(1)} %constant_dynamic-update-slice_fusion.4.p0), channel_id=1, source_target_pairs={{0,1},{1,0},{2,3},{3,2},{4,5},{5,4},{6,7},{7,6},{8,9},{9,8},{10,11... | collective-permute-start | bytes 2801672 | tf_op jit(solution)/shard_map/ppermute | solution.py:79
  47.6 13.4 %collective-permute-start.10 = (bf16[2,96,768]{2,1,0:T(8,128)(2,1)S(1)}, bf16[2,96,768]{2,1,0:T(8,128)(2,1)S(1)}, u32[]{:S(2)}, u32[]{:S(2)}) collective-permute-start(bf16[2,96,768]{2,1,0:T(8,128)(2,1)S(1)} %constant_dynamic-update-slice_fusion.8), channel_id=1, source_target_pairs={{0,8},{1,9},{2,10},{3,11},{4,12},{5,13},{6,14},{7,15},{8,0},{9,1},... | collective-permute-start | bytes 884744 | tf_op jit(solution)/shard_map/ppermute | solution.py:72
  55.1 56.9 %collective-permute-start.12 = (bf16[8,24,3840]{2,1,0:T(8,128)(2,1)}, bf16[8,24,3840]{2,1,0:T(8,128)(2,1)}, u32[]{:S(2)}, u32[]{:S(2)}) collective-permute-start(bf16[8,24,3840]{2,1,0:T(8,128)(2,1)} %constant_dynamic-update-slice_fusion.10.refs_0_), channel_id=1, source_target_pairs={{0,1},{1,0},{2,3},{3,2},{4,5},{5,4},{6,7},{7,6},{8,9},{9,8},{10,11... | collective-permute-start | bytes 4423688 | tf_op jit(solution)/shard_map/ppermute | solution.py:79
  55.6 25.9 %collective-permute-start.11 = (bf16[8,24,3840]{2,1,0:T(8,128)(2,1)}, bf16[8,24,3840]{2,1,0:T(8,128)(2,1)S(1)}, u32[]{:S(2)}, u32[]{:S(2)}) collective-permute-start(bf16[8,24,3840]{2,1,0:T(8,128)(2,1)} %constant_dynamic-update-slice_fusion.10.refs_0_), channel_id=1, source_target_pairs={{0,4},{1,3},{2,6},{3,1},{4,0},{5,7},{6,2},{7,5},{8,12},{9,11},{10,... | collective-permute-start | bytes 4423688 | tf_op jit(solution)/shard_map/ppermute | solution.py:72
  61.1 34.6 %collective-permute-start.14 = (bf16[4,96,768]{2,1,0:T(8,128)(2,1)S(1)}, bf16[4,96,768]{2,1,0:T(8,128)(2,1)S(1)}, u32[]{:S(2)}, u32[]{:S(2)}) collective-permute-start(bf16[4,96,768]{2,1,0:T(8,128)(2,1)S(1)} %constant_dynamic-update-slice_fusion.12), channel_id=1, source_target_pairs={{0,2},{1,5},{2,0},{3,7},{4,6},{5,1},{6,4},{7,3},{8,10},{9,13},{10,... | collective-permute-start | bytes 1769480 | tf_op jit(solution)/shard_map/ppermute | solution.py:72
  81.5 30.5 %collective-permute-start.13 = (bf16[8,24,3840]{2,1,0:T(8,128)(2,1)S(1)}, bf16[8,24,3840]{2,1,0:T(8,128)(2,1)S(1)}, u32[]{:S(2)}, u32[]{:S(2)}) collective-permute-start(bf16[8,24,3840]{2,1,0:T(8,128)(2,1)S(1)} %collective-permute-done.11.refs_1_), channel_id=1, source_target_pairs={{0,1},{1,0},{2,3},{3,2},{4,5},{5,4},{6,7},{7,6},{8,9},{9,8},{10,11... | collective-permute-start | bytes 4423688 | tf_op jit(solution)/shard_map/ppermute | solution.py:79
  95.7 16.3 %collective-permute-start.15 = (bf16[8,96,768]{2,1,0:T(8,128)(2,1)S(1)}, bf16[8,96,768]{2,1,0:T(8,128)(2,1)S(1)}, u32[]{:S(2)}, u32[]{:S(2)}) collective-permute-start(bf16[8,96,768]{2,1,0:T(8,128)(2,1)S(1)} %constant_dynamic-update-slice_fusion.14.refs_0_), channel_id=1, source_target_pairs={{0,4},{1,3},{2,6},{3,1},{4,0},{5,7},{6,2},{7,5},{8,12},{9,11},{10,... | collective-permute-start | bytes 3538952 | tf_op jit(solution)/shard_map/ppermute | solution.py:72
  97.3 39.9 %collective-permute-start.16 = (bf16[8,96,768]{2,1,0:T(8,128)(2,1)S(1)}, bf16[8,96,768]{2,1,0:T(8,128)(2,1)S(1)}, u32[]{:S(2)}, u32[]{:S(2)}) collective-permute-start(bf16[8,96,768]{2,1,0:T(8,128)(2,1)S(1)} %constant_dynamic-update-slice_fusion.14.refs_0_), channel_id=1, source_target_pairs={{0,1},{1,0},{2,3},{3,2},{4,5},{5,4},{6,7},{7,6},{8,9},{9,8},{10,11... | collective-permute-start | bytes 3538952 | tf_op jit(solution)/shard_map/ppermute | solution.py:79
  112.0 25.2 %collective-permute-start.17 = (bf16[8,96,768]{2,1,0:T(8,128)(2,1)S(1)}, bf16[8,96,768]{2,1,0:T(8,128)(2,1)S(1)}, u32[]{:S(2)}, u32[]{:S(2)}) collective-permute-start(bf16[8,96,768]{2,1,0:T(8,128)(2,1)S(1)} %collective-permute-done.15.refs_1_), channel_id=1, source_target_pairs={{0,1},{1,0},{2,3},{3,2},{4,5},{5,4},{6,7},{7,6},{8,9},{9,8},{10,11... | collective-permute-start | bytes 3538952 | tf_op jit(solution)/shard_map/ppermute | solution.py:79
  149.4 17.6 %collective-permute-start.20 = (bf16[8,96,768]{2,1,0:T(8,128)(2,1)}, bf16[8,96,768]{2,1,0:T(8,128)(2,1)}, u32[]{:S(2)}, u32[]{:S(2)}) collective-permute-start(bf16[8,96,768]{2,1,0:T(8,128)(2,1)} %add_convert_fusion.1), channel_id=1, source_target_pairs={{0,4},{1,3},{2,6},{3,1},{4,0},{5,7},{6,2},{7,5},{8,12},{9,11},{10,... | collective-permute-start | bytes 3538952 | tf_op jit(solution)/shard_map/ppermute | solution.py:113
  166.5 14.9 %collective-permute-start.21 = (bf16[16,24,768]{2,1,0:T(8,128)(2,1)S(1)}, bf16[16,24,768]{2,1,0:T(8,128)(2,1)S(1)}, u32[]{:S(2)}, u32[]{:S(2)}) collective-permute-start(bf16[16,24,768]{2,1,0:T(8,128)(2,1)S(1)} %get-tuple-element.339), channel_id=1, source_target_pairs={{0,1},{1,0},{2,3},{3,2},{4,5},{5,4},{6,7},{7,6},{8,9},{9,8},{10,11... | collective-permute-start | bytes 1769480 | tf_op jit(solution)/shard_map/ppermute | solution.py:93
  168.3 11.9 %collective-permute-start.23 = (bf16[4,96,768]{2,1,0:T(8,128)(2,1)S(1)}, bf16[4,96,768]{2,1,0:T(8,128)(2,1)S(1)}, u32[]{:S(2)}, u32[]{:S(2)}) collective-permute-start(bf16[4,96,768]{2,1,0:T(8,128)(2,1)S(1)} %add_convert_fusion.3), channel_id=1, source_target_pairs={{0,2},{1,5},{2,0},{3,7},{4,6},{5,1},{6,4},{7,3},{8,10},{9,13},{10,... | collective-permute-start | bytes 1769480 | tf_op jit(solution)/shard_map/ppermute | solution.py:113
  179.6 19.4 %collective-permute-start.27 = (bf16[8,24,3840]{2,1,0:T(8,128)(2,1)S(1)}, bf16[8,24,3840]{2,1,0:T(8,128)(2,1)S(1)}, u32[]{:S(2)}, u32[]{:S(2)}) collective-permute-start(bf16[8,24,3840]{2,1,0:T(8,128)(2,1)S(1)} %add_convert_fusion), channel_id=1, source_target_pairs={{0,4},{1,3},{2,6},{3,1},{4,0},{5,7},{6,2},{7,5},{8,12},{9,11},{10,... | collective-permute-start | bytes 4423688 | tf_op jit(solution)/shard_map/ppermute | solution.py:113
  181.3 18.7 %collective-permute-start.26 = (bf16[2,96,768]{2,1,0:T(8,128)(2,1)S(1)}, bf16[2,96,768]{2,1,0:T(8,128)(2,1)S(1)}, u32[]{:S(2)}, u32[]{:S(2)}) collective-permute-start(bf16[2,96,768]{2,1,0:T(8,128)(2,1)S(1)} %add_convert_fusion.8), channel_id=1, source_target_pairs={{0,8},{1,9},{2,10},{3,11},{4,12},{5,13},{6,14},{7,15},{8,0},{9,1},... | collective-permute-start | bytes 884744 | tf_op jit(solution)/shard_map/ppermute | solution.py:113
  181.8 27.3 %collective-permute-start.25 = (bf16[8,24,1536]{2,1,0:T(8,128)(2,1)S(1)}, bf16[8,24,1536]{2,1,0:T(8,128)(2,1)S(1)}, u32[]{:S(2)}, u32[]{:S(2)}) collective-permute-start(bf16[8,24,1536]{2,1,0:T(8,128)(2,1)S(1)} %pad_maximum_fusion), channel_id=1, source_target_pairs={{0,4},{1,3},{2,6},{3,1},{4,0},{5,7},{6,2},{7,5},{8,12},{9,11},{10,... | collective-permute-start | bytes 1769480 | tf_op jit(solution)/shard_map/ppermute | solution.py:113
  195.3 14.5 %collective-permute-start.24 = (bf16[16,24,896]{2,1,0:T(8,128)(2,1)S(1)}, bf16[16,24,896]{2,1,0:T(8,128)(2,1)S(1)}, u32[]{:S(2)}, u32[]{:S(2)}) collective-permute-start(bf16[16,24,896]{2,1,0:T(8,128)(2,1)S(1)} %get-tuple-element.398), channel_id=1, source_target_pairs={{0,1},{1,0},{2,3},{3,2},{4,5},{5,4},{6,7},{7,6},{8,9},{9,8},{10,11... | collective-permute-start | bytes 2064392 | tf_op jit(solution)/shard_map/ppermute | solution.py:93
  199.4 16.1 %collective-permute-start.30 = (bf16[4,24,3840]{2,1,0:T(8,128)(2,1)S(1)}, bf16[4,24,3840]{2,1,0:T(8,128)(2,1)S(1)}, u32[]{:S(2)}, u32[]{:S(2)}) collective-permute-start(bf16[4,24,3840]{2,1,0:T(8,128)(2,1)S(1)} %add_convert_fusion.2), channel_id=1, source_target_pairs={{0,2},{1,5},{2,0},{3,7},{4,6},{5,1},{6,4},{7,3},{8,10},{9,13},{10,... | collective-permute-start | bytes 2211848 | tf_op jit(solution)/shard_map/ppermute | solution.py:113
  229.6 15.6 %collective-permute-start.38 = (bf16[1,96,768]{2,1,0:T(8,128)(2,1)S(1)}, bf16[1,96,768]{2,1,0:T(8,128)(2,1)S(1)}, u32[]{:S(2)}, u32[]{:S(2)}) collective-permute-start(bf16[1,96,768]{2,1,0:T(8,128)(2,1)S(1)} %add_convert_fusion.11), channel_id=1, source_target_pairs={{0,16},{1,17},{2,18},{3,19},{4,20},{5,21},{6,22},{7,23},{8,24},{9,... | collective-permute-start | bytes 442376 | tf_op jit(solution)/shard_map/ppermute | solution.py:113
  231.9 15.0 %collective-permute-start.37 = (bf16[1,24,1536]{2,1,0:T(8,128)(2,1)S(1)}, bf16[1,24,1536]{2,1,0:T(8,128)(2,1)S(1)}, u32[]{:S(2)}, u32[]{:S(2)}) collective-permute-start(bf16[1,24,1536]{2,1,0:T(8,128)(2,1)S(1)} %fusion.6), channel_id=1, source_target_pairs={{0,16},{1,17},{2,18},{3,19},{4,20},{5,21},{6,22},{7,23},{8,24},{9,... | collective-permute-start | bytes 221192 | tf_op jit(solution)/shard_map/ppermute | solution.py:113
  232.5 17.4 %collective-permute-start.36 = (bf16[1,24,3840]{2,1,0:T(8,128)(2,1)S(1)}, bf16[1,24,3840]{2,1,0:T(8,128)(2,1)S(1)}, u32[]{:S(2)}, u32[]{:S(2)}) collective-permute-start(bf16[1,24,3840]{2,1,0:T(8,128)(2,1)S(1)} %add_convert_fusion.9), channel_id=1, source_target_pairs={{0,16},{1,17},{2,18},{3,19},{4,20},{5,21},{6,22},{7,23},{8,24},{9,... | collective-permute-start | bytes 552968 | tf_op jit(solution)/shard_map/ppermute | solution.py:113
  234.9 15.5 %collective-permute-start.35 = (bf16[1,24,896]{2,1,0:T(8,128)(2,1)S(1)}, bf16[1,24,896]{2,1,0:T(8,128)(2,1)S(1)}, u32[]{:S(2)}, u32[]{:S(2)}) collective-permute-start(bf16[1,24,896]{2,1,0:T(8,128)(2,1)S(1)} %add_convert_fusion.13), channel_id=1, source_target_pairs={{0,16},{1,17},{2,18},{3,19},{4,20},{5,21},{6,22},{7,23},{8,24},{9,... | collective-permute-start | bytes 129032 | tf_op jit(solution)/shard_map/ppermute | solution.py:113
  (36 other events, 398.3 us)
